TPU v7x, 256 devices: a whole 4x4x8 slice. The times are simulated.
256 devices in a mesh: len: 64 (over z, x, core), hgt: 4 (over y).
Axes of the slice: x: 4, y: 4, z: 8, core: 2. Of those that a mesh axis runs over, the one named last changes fastest.
Arguments:
- slave_disp: bfloat16 [256, 16, 96, 256], P('len', 'hgt'), may hold values from -6 to 6
- master_disp: bfloat16 [256, 16, 96, 256], P('len', 'hgt'), may hold values from -6 to 6
- quad_coords: float32 [64, 4, 64, 4, 256], P('len', 'hgt'), may hold values from 0 to 1
- quad_weights: float32 [64, 4, 64, 256], P('len', 'hgt'), may hold values from 0.0005 to 0.02
- pair_count: int32 [64, 4], P('len', 'hgt'), may hold values from 24 to 64, as said below
- slave_face: int32 [64, 4, 64], P('len', 'hgt'), may hold values from 0 to 15
- master_row: int32 [64, 4, 64], P('len', 'hgt'), may hold values from 0 to 255, as said below
- master_col: int32 [64, 4, 64], P('len', 'hgt'), may hold values from 0 to 15, as said below
- active: int32 [64, 4, 64], P('len', 'hgt'), may hold values 0 or 1
Outputs:
- master_force: float32 [256, 16, 96, 256], P('len', 'hgt')
- slave_multiplier: float32 [256, 16, 96, 256], P('len', 'hgt')
Inputs may be any that keep to these rules, and one draw needn't show every extreme that they name: `pair_count`: some band cell has all 64 slots live in count in every draw; every other cell has between 24 and 56. `master_row`: A pair's master face lies in its own band cell's block of 4 rows or in the block beside it along the length, within the grid. `master_col`: A pair's master face lies in its own band cell's block of 4 columns or in the block beside it along the height, within the grid.
All inputs are finite; a program needn't handle non-finite values. No bound on the sum of `active` on one device may be relied on, other than what follows from the above.
Results may differ from a plain program's by a relative error of at most 0.002.
Values may be sent and summed in bfloat16 or wider, within the bound.
A program may use at most 128 MiB of HBM per device.

v0:
```python
import jax
import jax.numpy as jnp
from jax import lax
from jax.sharding import PartitionSpec as P

ORDER = 16
PAIR_BLOCK = 32


def shifted(block, axis, distance):
    devices = range(lax.axis_size(axis))
    route = [(i - distance, i) for i in devices if i - distance in devices]
    return lax.ppermute(block, axis, route)


def padded(value, sides, width):
    for axis, dim in sides:
        size, length = (lax.axis_size(axis), value.shape[dim])
        up = [(i, (i + 1) % size) for i in range(size - 1)]
        down = [(j, i) for i, j in up]
        last = lax.slice_in_dim(value, length - width, length, axis=dim)
        leading = lax.slice_in_dim(value, 0, width, axis=dim)
        before = lax.ppermute(last, axis, up)
        after = lax.ppermute(leading, axis, down)
        value = jnp.concatenate([before, value, after], axis=dim)
    return value


def face_basis(points, basis_order):
    mode_numbers = jnp.arange(basis_order, dtype=jnp.float32)
    return jnp.cos(jnp.pi * mode_numbers[None, :, None] * points[:, None, :])


def coupling(coords_block, weights_block, basis_order):
    pairs = coords_block.shape[0]
    quad_pts = coords_block.shape[2]
    slave_first = face_basis(coords_block[:, 0], basis_order)
    slave_second = face_basis(coords_block[:, 1], basis_order)
    master_first = face_basis(coords_block[:, 2], basis_order)
    master_second = face_basis(coords_block[:, 3], basis_order)
    slave_table = (slave_first[:, :, None, :] * slave_second[:, None, :, :]).reshape(
        pairs, basis_order * basis_order, quad_pts
    )
    master_table = (master_first[:, :, None, :] * master_second[:, None, :, :]).reshape(
        pairs, basis_order * basis_order, quad_pts
    )
    mortar = jnp.einsum(
        "pjq,pkq->pjk",
        slave_table,
        master_table * weights_block[:, None, :],
        precision=lax.Precision.HIGHEST,
    )
    dual_diag = jnp.sum(weights_block[:, None, :] * slave_table * slave_table, axis=2)
    return (mortar.astype(jnp.bfloat16), dual_diag)


def fold_len(field):
    third = field.shape[0] // 3
    from_above = shifted(field[:third], "len", -1)
    from_below = shifted(field[2 * third :], "len", 1)
    return field[third : 2 * third] + from_above + from_below


def fold_hgt(field):
    third = field.shape[1] // 3
    from_above = shifted(field[:, :third], "hgt", -1)
    from_below = shifted(field[:, 2 * third :], "hgt", 1)
    return field[:, third : 2 * third] + from_above + from_below


def body(
    slave_disp,
    master_disp,
    quad_coords,
    quad_weights,
    pair_count,
    slave_face,
    master_row,
    master_col,
    active,
):
    side = master_disp.shape[0]
    channels = master_disp.shape[2]
    nodes = master_disp.shape[3]
    capacity = quad_coords.shape[2]
    coords_local = quad_coords[0, 0]
    weights_local = quad_weights[0, 0]
    live_count = pair_count[0, 0]
    block_total = (live_count + PAIR_BLOCK - 1) // PAIR_BLOCK
    slot_ids = jnp.arange(capacity, dtype=jnp.int32)
    live = ((slot_ids < live_count) & (active[0, 0] == 1)).astype(jnp.float32)
    band_len = lax.axis_index("len")
    band_hgt = lax.axis_index("hgt")
    slave_index = slave_face[0, 0]
    master_index = (
        (master_row[0, 0] - (band_len - 1) * side) * (3 * side)
        + master_col[0, 0]
        - (band_hgt - 1) * side
    )

    def blocks_of(first_slot):
        coords_block = lax.dynamic_slice_in_dim(coords_local, first_slot, PAIR_BLOCK, 0)
        weights_block = lax.dynamic_slice_in_dim(weights_local, first_slot, PAIR_BLOCK, 0)
        return coupling(coords_block, weights_block, ORDER)

    window = padded(master_disp, (("len", 0), ("hgt", 1)), side)
    window_rows = window.reshape(9 * side * side, channels, nodes)
    slave_rows = slave_disp.reshape(side * side, channels, nodes)

    def visit(block_index, totals):
        forces, slave_sum = totals
        first_slot = block_index * PAIR_BLOCK
        mortar, dual_diag = blocks_of(first_slot)
        live_block = lax.dynamic_slice_in_dim(live, first_slot, PAIR_BLOCK, 0)
        sidx = lax.dynamic_slice_in_dim(slave_index, first_slot, PAIR_BLOCK, 0)
        midx = lax.dynamic_slice_in_dim(master_index, first_slot, PAIR_BLOCK, 0)
        master_part = window_rows[midx]
        slave_part = slave_rows[sidx].astype(jnp.float32)
        projected = jnp.einsum(
            "pck,pjk->pcj", master_part, mortar, preferred_element_type=jnp.float32
        )
        weighted_gap = slave_part * dual_diag[:, None, :] - projected
        multiplier = live_block[:, None, None] * weighted_gap / dual_diag[:, None, :]
        multiplier_b = multiplier.astype(jnp.bfloat16)
        push = jnp.einsum("pcj,pjk->pck", multiplier_b, mortar, preferred_element_type=jnp.float32)
        return (forces.at[midx].add(push), slave_sum.at[sidx].add(multiplier))

    start_totals = (
        jnp.zeros((9 * side * side, channels, nodes), jnp.float32),
        jnp.zeros((side * side, channels, nodes), jnp.float32),
    )
    forces, slave_sum = lax.fori_loop(0, block_total, visit, start_totals)
    force_window = forces.reshape(3 * side, 3 * side, channels, nodes)
    master_force = fold_hgt(fold_len(force_window))
    return (master_force, slave_sum.reshape(side, side, channels, nodes))


def solution(mesh):
    in_specs = (
        P("len", "hgt", None, None),
        P("len", "hgt", None, None),
        P("len", "hgt", None, None, None),
        P("len", "hgt", None, None),
        P("len", "hgt"),
        P("len", "hgt", None),
        P("len", "hgt", None),
        P("len", "hgt", None),
        P("len", "hgt", None),
    )
    out_specs = (P("len", "hgt", None, None), P("len", "hgt", None, None))
    return jax.shard_map(body, mesh=mesh, in_specs=in_specs, out_specs=out_specs, check_vma=False)
```

profile of v0, /device:TPU:111, one launch (start us, length us, event | category | flops | bytes accessed | tf_op | source)
XLA Modules:
  0.0 310.6 jit_solution(2564223105124205931)
XLA Ops:
  0.7 5.4 %collective-permute-start = (bf16[4,4,96,256]{3,2,1,0:T(8,128)(2,1)}, bf16[4,4,96,256]{3,2,1,0:T(8,128)(2,1)S(1)}, u32[]{:S(2)}, u32[]{:S(2)}) collective-permute-start(bf16[4,4,96,256]{3,2,1,0:T(8,128)(2,1)} %param.12), channel_id=1, source_target_pairs={{0,4},{4,8},{8,12},{12,16},{16,20},{20,24},{24,28},{28,32},{32,36}... | collective-permute-start | bytes 2359304 | tf_op jit(solution)/shard_map/ppermute | solution.py:23
  8.0 7.3 %collective-permute-done = bf16[4,4,96,256]{3,2,1,0:T(8,128)(2,1)S(1)} collective-permute-done((bf16[4,4,96,256]{3,2,1,0:T(8,128)(2,1)}, bf16[4,4,96,256]{3,2,1,0:T(8,128)(2,1)S(1)}, u32[]{:S(2)}, u32[]{:S(2)}) %collective-permute-start) | collective-permute-done | bytes 786464 | tf_op jit(solution)/shard_map/ppermute | solution.py:23
  16.5 6.4 %collective-permute-done.1 = bf16[4,4,96,256]{3,2,1,0:T(8,128)(2,1)S(1)} collective-permute-done((bf16[4,4,96,256]{3,2,1,0:T(8,128)(2,1)}, bf16[4,4,96,256]{3,2,1,0:T(8,128)(2,1)S(1)}, u32[]{:S(2)}, u32[]{:S(2)}) %collective-permute-start.1) | collective-permute-done | bytes 786464 | tf_op jit(solution)/shard_map/ppermute | solution.py:24
  22.9 3.2 %collective-permute-start.2 = (bf16[12,4,96,256]{3,2,1,0:T(8,128)(2,1)S(1)}, bf16[12,4,96,256]{3,2,1,0:T(8,128)(2,1)}, u32[]{:S(2)}, u32[]{:S(2)}) collective-permute-start(bf16[12,4,96,256]{3,2,1,0:T(8,128)(2,1)S(1)} %constant_dynamic-update-slice_fusion), channel_id=1, source_target_pairs={{0,1},{1,2},{2,3},{4,5},{5,6},{6,7},{8,9},{9,10},{10,11},{12,13},{... | collective-permute-start | bytes 7077896 | tf_op jit(solution)/shard_map/ppermute | solution.py:23
  26.2 3.5 %collective-permute-start.3 = (bf16[12,4,96,256]{3,2,1,0:T(8,128)(2,1)S(1)}, bf16[12,4,96,256]{3,2,1,0:T(8,128)(2,1)}, u32[]{:S(2)}, u32[]{:S(2)}) collective-permute-start(bf16[12,4,96,256]{3,2,1,0:T(8,128)(2,1)S(1)} %constant_dynamic-update-slice_fusion), channel_id=1, source_target_pairs={{1,0},{2,1},{3,2},{5,4},{6,5},{7,6},{9,8},{10,9},{11,10},{13,12},{... | collective-permute-start | bytes 7077896 | tf_op jit(solution)/shard_map/ppermute | solution.py:24
  30.5 41.9 %collective-permute-done.2 = bf16[12,4,96,256]{3,2,1,0:T(8,128)(2,1)} collective-permute-done((bf16[12,4,96,256]{3,2,1,0:T(8,128)(2,1)S(1)}, bf16[12,4,96,256]{3,2,1,0:T(8,128)(2,1)}, u32[]{:S(2)}, u32[]{:S(2)}) %collective-permute-start.2) | collective-permute-done | bytes 2359328 | tf_op jit(solution)/shard_map/ppermute | solution.py:23
  72.4 3.5 %collective-permute-done.3 = bf16[12,4,96,256]{3,2,1,0:T(8,128)(2,1)} collective-permute-done((bf16[12,4,96,256]{3,2,1,0:T(8,128)(2,1)S(1)}, bf16[12,4,96,256]{3,2,1,0:T(8,128)(2,1)}, u32[]{:S(2)}, u32[]{:S(2)}) %collective-permute-start.3) | collective-permute-done | bytes 2359328 | tf_op jit(solution)/shard_map/ppermute | solution.py:24
  75.8 5.8 %pad_maximum_fusion = bf16[12,12,96,256]{3,2,1,0:T(8,128)(2,1)} fusion(bf16[12,4,96,256]{3,2,1,0:T(8,128)(2,1)} %collective-permute-done.3, bf16[12,4,96,256]{3,2,1,0:T(8,128)(2,1)S(1)} %constant_dynamic-update-slice_fusion, bf16[12,4,96,256]{3,2,1,0:T(8,128)(2,1)} %collective-permute-done.2), kind=kLoop, calls=%fused_computation.27 | loop fusion | flops 7077888 | bytes 14155776 | tf_op jit(solution)/shard_map/concatenate | solution.py:25
  81.6 6.8 %broadcast_in_dim.8 = f32[144,96,256]{2,1,0:T(8,128)} broadcast(f32[]{:T(128)} %constant.46.clone.1), dimensions={} | broadcast | bytes 14155780 | tf_op jit(solution)/shard_map/broadcast_in_dim | solution.py:129
  89.8 105.1 %while.12 = (s32[]{:T(128)}, f32[144,96,256]{2,1,0:T(8,128)}, f32[16,96,256]{2,1,0:T(8,128)}, s32[]{:T(128)}, s32[64]{0:T(128)S(1)}, /*index=5*/f32[64]{0:T(128)...) while((s32[]{:T(128)}, f32[144,96,256]{2,1,0:T(8,128)}, ...), condition=%wide.region_4.5_spmd, body=%wide.region_0.4_spmd.sunk | while | flops 7269246976 | bytes 122366008 | solution.py:132
  89.8 6.7 %multiply_cosine_fusion.5 = (f32[32,16,256]{2,1,0:T(8,128)S(1)}, f32[32,16,256]{2,1,0:T(8,128)S(1)}, f32[32,16,256]{2,1,0:T(8,128)S(1)}, f32[32,16,256]{2,1,0:T(8,128)S(1)}) fusion(f32[32,256]{1,0:T(8,128)S(1)} %get-tuple-element.183, f32[16]{0:T(128)S(1)} %iota_multiply_fusion.2, f32[32,256]{1,0:T(8,128)S(1)} %get-tuple-element.184, ...), kind=kLoop, calls=%fused_computation.14.clone.1 | loop fusion | flops 524288 | bytes 2228288 | tf_op jit(solution)/shard_map/while/body/cos | solution.py:31
  100.8 10.3 %convolution_convert_fusion.2 = bf16[32,256,256]{2,1,0:T(8,128)(2,1)} fusion(f32[32,256,256]{2,1,0:T(8,128)S(1)} %bitcast.55, f32[32,256,256]{2,1,0:T(8,128)S(1)} %bitcast_multiply_fusion.2), kind=kOutput, calls=%fused_computation.10.clone.1 | convolution fusion | flops 6444548096 | bytes 20971520 | tf_op jit(solution)/shard_map/while/body/pjq,pkq->pjk/dot_general | solution.py:47
  111.4 2.9 gather_fusion
  114.3 4.8 %gather_fusion.1 = bf16[32,96,256]{2,1,0:T(8,128)(2,1)} fusion(bf16[144,96,256]{2,1,0:T(8,128)(2,1)} %get-tuple-element.240, s32[1024]{0:T(1024)S(1)} %pad_clamp_fusion.5), kind=kCustom, calls=%fused_computation.1.clone.1 | custom fusion | bytes 3145856 | tf_op jit(solution)/shard_map/while/body/gather | solution.py:117
  119.2 4.7 %multiply_divide_fusion.2 = f32[32,96,256]{2,1,0:T(8,128)S(1)} fusion(bf16[32,96,256]{2,1,0:T(8,128)(2,1)} %gather_fusion, bf16[32,96,256]{2,1,0:T(8,128)(2,1)} %gather_fusion.1, bf16[32,256,256]{2,1,0:T(8,128)(2,1)} %convolution_convert_fusion.2, f32[32,256]{1,0:T(8,128)S(1)} %copy.22, f32[32]{0:T(128)S(1)} %dynamic_slice.23), kind=kOutput, calls=%fused_computation.9.clone.1 | convolution fusion | flops 406585344 | bytes 10518656 | tf_op jit(solution)/shard_map/while/body/pck,pjk->pcj/dot_general | solution.py:119
  123.9 2.5 fusion.27
  126.5 8.6 %scatter_fusion = f32[144,96,256]{2,1,0:T(8,128)} fusion(f32[144,96,256]{2,1,0:T(8,128)} %get-tuple-element.213, s32[32]{0:T(128)S(1)} %get-tuple-element.182, f32[32,96,256]{2,1,0:T(8,128)} %fusion.27), kind=kCustom, calls=%fused_computation.2.clone.1 | custom fusion | flops 786432 | bytes 9437312 | tf_op jit(solution)/shard_map/while/body/scatter-add | solution.py:126
  135.1 7.2 %scatter_fusion.1 = f32[16,96,256]{2,1,0:T(8,128)} fusion(f32[16,96,256]{2,1,0:T(8,128)} %get-tuple-element.214, s32[32]{0:T(128)S(1)} %get-tuple-element.192, f32[32,96,256]{2,1,0:T(8,128)S(1)} %multiply_divide_fusion.2), kind=kCustom, calls=%fused_computation.3.clone.1 | custom fusion | flops 786432 | bytes 9437312 | tf_op jit(solution)/shard_map/while/body/scatter-add | solution.py:126
  142.3 6.7 %multiply_cosine_fusion.5 = (f32[32,16,256]{2,1,0:T(8,128)S(1)}, f32[32,16,256]{2,1,0:T(8,128)S(1)}, f32[32,16,256]{2,1,0:T(8,128)S(1)}, f32[32,16,256]{2,1,0:T(8,128)S(1)}) fusion(f32[32,256]{1,0:T(8,128)S(1)} %get-tuple-element.183, f32[16]{0:T(128)S(1)} %iota_multiply_fusion.2, f32[32,256]{1,0:T(8,128)S(1)} %get-tuple-element.184, ...), kind=kLoop, calls=%fused_computation.14.clone.1 | loop fusion | flops 524288 | bytes 2228288 | tf_op jit(solution)/shard_map/while/body/cos | solution.py:31
  153.2 10.3 %convolution_convert_fusion.2 = bf16[32,256,256]{2,1,0:T(8,128)(2,1)} fusion(f32[32,256,256]{2,1,0:T(8,128)S(1)} %bitcast.55, f32[32,256,256]{2,1,0:T(8,128)S(1)} %bitcast_multiply_fusion.2), kind=kOutput, calls=%fused_computation.10.clone.1 | convolution fusion | flops 6444548096 | bytes 20971520 | tf_op jit(solution)/shard_map/while/body/pjq,pkq->pjk/dot_general | solution.py:47
  163.8 2.9 gather_fusion
  166.8 4.8 %gather_fusion.1 = bf16[32,96,256]{2,1,0:T(8,128)(2,1)} fusion(bf16[144,96,256]{2,1,0:T(8,128)(2,1)} %get-tuple-element.240, s32[1024]{0:T(1024)S(1)} %pad_clamp_fusion.5), kind=kCustom, calls=%fused_computation.1.clone.1 | custom fusion | bytes 3145856 | tf_op jit(solution)/shard_map/while/body/gather | solution.py:117
  171.7 4.7 %multiply_divide_fusion.2 = f32[32,96,256]{2,1,0:T(8,128)S(1)} fusion(bf16[32,96,256]{2,1,0:T(8,128)(2,1)} %gather_fusion, bf16[32,96,256]{2,1,0:T(8,128)(2,1)} %gather_fusion.1, bf16[32,256,256]{2,1,0:T(8,128)(2,1)} %convolution_convert_fusion.2, f32[32,256]{1,0:T(8,128)S(1)} %copy.22, f32[32]{0:T(128)S(1)} %dynamic_slice.23), kind=kOutput, calls=%fused_computation.9.clone.1 | convolution fusion | flops 406585344 | bytes 10518656 | tf_op jit(solution)/shard_map/while/body/pck,pjk->pcj/dot_general | solution.py:119
  176.4 2.5 fusion.27
  178.9 8.6 %scatter_fusion = f32[144,96,256]{2,1,0:T(8,128)} fusion(f32[144,96,256]{2,1,0:T(8,128)} %get-tuple-element.213, s32[32]{0:T(128)S(1)} %get-tuple-element.182, f32[32,96,256]{2,1,0:T(8,128)} %fusion.27), kind=kCustom, calls=%fused_computation.2.clone.1 | custom fusion | flops 786432 | bytes 9437312 | tf_op jit(solution)/shard_map/while/body/scatter-add | solution.py:126
  187.5 7.3 %scatter_fusion.1 = f32[16,96,256]{2,1,0:T(8,128)} fusion(f32[16,96,256]{2,1,0:T(8,128)} %get-tuple-element.214, s32[32]{0:T(128)S(1)} %get-tuple-element.192, f32[32,96,256]{2,1,0:T(8,128)S(1)} %multiply_divide_fusion.2), kind=kCustom, calls=%fused_computation.3.clone.1 | custom fusion | flops 786432 | bytes 9437312 | tf_op jit(solution)/shard_map/while/body/scatter-add | solution.py:126
  194.8 10.7 %fusion.5 = (f32[48,96,256]{2,1,0:T(8,128)}, f32[48,96,256]{2,1,0:T(8,128)}, f32[48,96,256]{2,1,0:T(8,128)}) fusion(f32[144,96,256]{2,1,0:T(8,128)} %get-tuple-element.61), kind=kLoop, calls=%fused_computation.38 | loop fusion | bytes 28311552 | tf_op jit(solution)/shard_map/slice | solution.py:59
  207.4 7.0 %collective-permute-start.5 = (f32[4,12,96,256]{3,2,1,0:T(8,128)}, f32[4,12,96,256]{3,2,1,0:T(8,128)S(1)}, u32[]{:S(2)}, u32[]{:S(2)}) collective-permute-start(f32[4,12,96,256]{3,2,1,0:T(8,128)} %bitcast.60), channel_id=1, source_target_pairs={{0,4},{4,8},{8,12},{12,16},{16,20},{20,24},{24,28},{28,32},{32,36}... | collective-permute-start | bytes 14155784 | tf_op jit(solution)/shard_map/ppermute | solution.py:13
  214.4 50.1 %collective-permute-done.4 = f32[4,12,96,256]{3,2,1,0:T(8,128)S(1)} collective-permute-done((f32[4,12,96,256]{3,2,1,0:T(8,128)}, f32[4,12,96,256]{3,2,1,0:T(8,128)S(1)}, u32[]{:S(2)}, u32[]{:S(2)}) %collective-permute-start.4) | collective-permute-done | bytes 4718624 | tf_op jit(solution)/shard_map/ppermute | solution.py:13
  265.8 4.0 %add_add_fusion = f32[4,12,96,256]{3,2,1,0:T(8,128)S(1)} fusion(f32[4,12,96,256]{3,2,1,0:T(8,128)S(1)} %collective-permute-done.5, f32[4,12,96,256]{3,2,1,0:T(8,128)} %bitcast.58, f32[4,12,96,256]{3,2,1,0:T(8,128)S(1)} %collective-permute-done.4), kind=kLoop, calls=%fused_computation.28 | loop fusion | flops 2359296 | bytes 18874368 | tf_op jit(solution)/shard_map/add | solution.py:61
  270.1 3.4 %collective-permute-start.6 = (f32[4,4,96,256]{3,2,1,0:T(8,128)S(1)}, f32[4,4,96,256]{3,2,1,0:T(8,128)S(1)}, u32[]{:S(2)}, u32[]{:S(2)}) collective-permute-start(f32[4,4,96,256]{3,2,1,0:T(8,128)S(1)} %get-tuple-element.100), channel_id=1, source_target_pairs={{1,0},{2,1},{3,2},{5,4},{6,5},{7,6},{9,8},{10,9},{11,10},{13,12},{... | collective-permute-start | bytes 4718600 | tf_op jit(solution)/shard_map/ppermute | solution.py:13
  275.4 31.4 %collective-permute-done.6 = f32[4,4,96,256]{3,2,1,0:T(8,128)S(1)} collective-permute-done((f32[4,4,96,256]{3,2,1,0:T(8,128)S(1)}, f32[4,4,96,256]{3,2,1,0:T(8,128)S(1)}, u32[]{:S(2)}, u32[]{:S(2)}) %collective-permute-start.6) | collective-permute-done | bytes 1572896 | tf_op jit(solution)/shard_map/ppermute | solution.py:13
  (54 shorter events, 23.1 us)
Async XLA Ops:
  0.6 29.7 %copy-start.2 = (f32[1,1,64,4,256]{4,3,2,1,0:T(4,128)S(1)}, f32[1,1,64,4,256]{4,3,2,1,0:T(4,128)}, u32[]{:S(2)}) copy-start(f32[1,1,64,4,256]{4,3,2,1,0:T(4,128)} %param.13) | copy-start | bytes 786436
  0.6 29.8 %copy-start.6 = (s32[1,1,64]{2,1,0:T(1,128)S(1)}, s32[1,1,64]{2,1,0:T(1,128)}, u32[]{:S(2)}) copy-start(s32[1,1,64]{2,1,0:T(1,128)} %param.19) | copy-start | bytes 772
  0.7 29.8 %copy-start.5 = (s32[1,1,64]{2,1,0:T(1,128)S(1)}, s32[1,1,64]{2,1,0:T(1,128)}, u32[]{:S(2)}) copy-start(s32[1,1,64]{2,1,0:T(1,128)} %param.17) | copy-start | bytes 772
  0.7 29.8 %copy-start.4 = (s32[1,1,64]{2,1,0:T(1,128)S(1)}, s32[1,1,64]{2,1,0:T(1,128)}, u32[]{:S(2)}) copy-start(s32[1,1,64]{2,1,0:T(1,128)} %param.18) | copy-start | bytes 772
  0.7 14.6 %collective-permute-start = (bf16[4,4,96,256]{3,2,1,0:T(8,128)(2,1)}, bf16[4,4,96,256]{3,2,1,0:T(8,128)(2,1)S(1)}, u32[]{:S(2)}, u32[]{:S(2)}) collective-permute-start(bf16[4,4,96,256]{3,2,1,0:T(8,128)(2,1)} %param.12), channel_id=1, source_target_pairs={{0,4},{4,8},{8,12},{12,16},{16,20},{20,24},{24,28},{28,32},{32,36}... | collective-permute-start | bytes 2359304 | tf_op jit(solution)/shard_map/ppermute | solution.py:23
  6.0 16.8 %collective-permute-start.1 = (bf16[4,4,96,256]{3,2,1,0:T(8,128)(2,1)}, bf16[4,4,96,256]{3,2,1,0:T(8,128)(2,1)S(1)}, u32[]{:S(2)}, u32[]{:S(2)}) collective-permute-start(bf16[4,4,96,256]{3,2,1,0:T(8,128)(2,1)} %param.12), channel_id=1, source_target_pairs={{4,0},{8,4},{12,8},{16,12},{20,16},{24,20},{28,24},{32,28},{36,32}... | collective-permute-start | bytes 2359304 | tf_op jit(solution)/shard_map/ppermute | solution.py:24
  22.9 49.4 %collective-permute-start.2 = (bf16[12,4,96,256]{3,2,1,0:T(8,128)(2,1)S(1)}, bf16[12,4,96,256]{3,2,1,0:T(8,128)(2,1)}, u32[]{:S(2)}, u32[]{:S(2)}) collective-permute-start(bf16[12,4,96,256]{3,2,1,0:T(8,128)(2,1)S(1)} %constant_dynamic-update-slice_fusion), channel_id=1, source_target_pairs={{0,1},{1,2},{2,3},{4,5},{5,6},{6,7},{8,9},{9,10},{10,11},{12,13},{... | collective-permute-start | bytes 7077896 | tf_op jit(solution)/shard_map/ppermute | solution.py:23
  26.2 49.7 %collective-permute-start.3 = (bf16[12,4,96,256]{3,2,1,0:T(8,128)(2,1)S(1)}, bf16[12,4,96,256]{3,2,1,0:T(8,128)(2,1)}, u32[]{:S(2)}, u32[]{:S(2)}) collective-permute-start(bf16[12,4,96,256]{3,2,1,0:T(8,128)(2,1)S(1)} %constant_dynamic-update-slice_fusion), channel_id=1, source_target_pairs={{1,0},{2,1},{3,2},{5,4},{6,5},{7,6},{9,8},{10,9},{11,10},{13,12},{... | collective-permute-start | bytes 7077896 | tf_op jit(solution)/shard_map/ppermute | solution.py:24
  81.6 8.1 %copy-start.1 = (f32[1,1,64,256]{3,2,1,0:T(8,128)S(1)}, f32[1,1,64,256]{3,2,1,0:T(8,128)}, u32[]{:S(2)}) copy-start(f32[1,1,64,256]{3,2,1,0:T(8,128)} %param.14) | copy-start | bytes 196612
  81.6 8.1 %copy-start.3 = (s32[1,1,64]{2,1,0:T(1,128)S(1)}, s32[1,1,64]{2,1,0:T(1,128)}, u32[]{:S(2)}) copy-start(s32[1,1,64]{2,1,0:T(1,128)} %param.16) | copy-start | bytes 772
  119.2 4.7 %copy-start = (bf16[32,256,256]{2,1,0:T(8,128)(2,1)S(1)}, bf16[32,256,256]{2,1,0:T(8,128)(2,1)}, u32[]{:S(2)}) copy-start(bf16[32,256,256]{2,1,0:T(8,128)(2,1)} %convolution_convert_fusion.2) | copy-start | bytes 12582916 | tf_op jit(solution)/shard_map/while
  171.7 4.7 %copy-start = (bf16[32,256,256]{2,1,0:T(8,128)(2,1)S(1)}, bf16[32,256,256]{2,1,0:T(8,128)(2,1)}, u32[]{:S(2)}) copy-start(bf16[32,256,256]{2,1,0:T(8,128)(2,1)} %convolution_convert_fusion.2) | copy-start | bytes 12582916 | tf_op jit(solution)/shard_map/while
  205.5 59.0 %collective-permute-start.4 = (f32[4,12,96,256]{3,2,1,0:T(8,128)}, f32[4,12,96,256]{3,2,1,0:T(8,128)S(1)}, u32[]{:S(2)}, u32[]{:S(2)}) collective-permute-start(f32[4,12,96,256]{3,2,1,0:T(8,128)} %bitcast.61), channel_id=1, source_target_pairs={{4,0},{8,4},{12,8},{16,12},{20,16},{24,20},{28,24},{32,28},{36,32}... | collective-permute-start | bytes 14155784 | tf_op jit(solution)/shard_map/ppermute | solution.py:13
  207.4 58.3 %collective-permute-start.5 = (f32[4,12,96,256]{3,2,1,0:T(8,128)}, f32[4,12,96,256]{3,2,1,0:T(8,128)S(1)}, u32[]{:S(2)}, u32[]{:S(2)}) collective-permute-start(f32[4,12,96,256]{3,2,1,0:T(8,128)} %bitcast.60), channel_id=1, source_target_pairs={{0,4},{4,8},{8,12},{12,16},{16,20},{20,24},{24,28},{28,32},{32,36}... | collective-permute-start | bytes 14155784 | tf_op jit(solution)/shard_map/ppermute | solution.py:13
  270.1 36.7 %collective-permute-start.6 = (f32[4,4,96,256]{3,2,1,0:T(8,128)S(1)}, f32[4,4,96,256]{3,2,1,0:T(8,128)S(1)}, u32[]{:S(2)}, u32[]{:S(2)}) collective-permute-start(f32[4,4,96,256]{3,2,1,0:T(8,128)S(1)} %get-tuple-element.100), channel_id=1, source_target_pairs={{1,0},{2,1},{3,2},{5,4},{6,5},{7,6},{9,8},{10,9},{11,10},{13,12},{... | collective-permute-start | bytes 4718600 | tf_op jit(solution)/shard_map/ppermute | solution.py:13
  273.5 35.6 %collective-permute-start.7 = (f32[4,4,96,256]{3,2,1,0:T(8,128)S(1)}, f32[4,4,96,256]{3,2,1,0:T(8,128)S(1)}, u32[]{:S(2)}, u32[]{:S(2)}) collective-permute-start(f32[4,4,96,256]{3,2,1,0:T(8,128)S(1)} %get-tuple-element.101), channel_id=1, source_target_pairs={{0,1},{1,2},{2,3},{4,5},{5,6},{6,7},{8,9},{9,10},{10,11},{12,13},{... | collective-permute-start | bytes 4718600 | tf_op jit(solution)/shard_map/ppermute | solution.py:13
where the time goes:
time: 313 us; the launch traced here: 311 us
  waiting for transfers between devices  144 us (46%)
  other arithmetic  65 us (21%)
  local copies, waits for them, and re-layouts  36.7 us (12%)
  matrix products  35 us (11%)
  starting transfers between devices  28.2 us (9%)
    ppermute x4, waiting for transfers between devices, shifted(): return lax.ppermute(block, axis, route)  85.1 us
    ppermute x2, waiting for transfers between devices, padded(): before = lax.ppermute(last, axis, up)  49.2 us
    scatter-add x4, other arithmetic, visit(): return (forces.at[midx].add(push), slave_sum.at[sidx].add(multiplier))  31.7 us
    dot_general x2, matrix products, coupling(): jnp.einsum('pjq,pkq->pjk', slave_table, master_table * weights_block[:, N...  20.6 us
    ppermute x4, starting transfers between devices, shifted(): return lax.ppermute(block, axis, route)  14.2 us
    cos x2, other arithmetic, face_basis(): return jnp.cos(jnp.pi * mode_numbers[None, :, None] * points[:, None, :])  13.4 us
    slice x1, local copies, waits for them, and re-layouts, fold_len(): from_above = shifted(field[:third], 'len', -1)  10.7 us
    ppermute x2, waiting for transfers between devices, padded(): after = lax.ppermute(leading, axis, down)  9.86 us
  transfers between devices with their start and end apart: 8, of which 8 were waited for; matrix products, arithmetic and copies ran while one was open for 0% of the time, Pallas kernels for 0%

commit v1 on v0

v1 whole, which is shorter than its diff:
```python
import functools

import jax
import jax.numpy as jnp
from jax import lax
from jax.experimental import pallas as pl
from jax.experimental.pallas import tpu as pltpu
from jax.sharding import PartitionSpec as P

ORDER = 16
NODES = 256
CHANNELS = 96
FACES = 16
PAIRS = 64
GROUP = 16
LOCK_A = 4
LOCK_B = 8
CHUNKS = 4
PART = FACES // CHUNKS
EXTRA = 1
F32, BF16 = jnp.float32, jnp.bfloat16
MESH = pl.DeviceIdType.MESH
NT = (((1,), (1,)), ((), ()))
NN = (((1,), (0,)), ((), ()))

OWN, PARTNER, OTHER = range(3)
DOWN, UP, MID = range(3)
BLOCKS = 9
SPOTS = BLOCKS * FACES

AT_PAIR, AT_MASTER, AT_SLAVE, AT_LIVE, AT_KEEP = (i * PAIRS for i in range(5))
AT_LAST = 5 * PAIRS
AT_HAS = AT_LAST + SPOTS


def cos_pi(turns):
    reduced = turns - 2.0 * jnp.round(turns * 0.5)
    s = (0.5 - jnp.abs(reduced)) - 1.4e-8
    s2 = s * s
    p = jnp.float32(-0.00737043)
    for c in (0.082145887, -0.59926453, 2.5501640, -5.1677128, 3.1415927):
        p = p * s2 + jnp.float32(c)
    return p * s


def split(value):
    high = value.astype(BF16)
    return high, (value - high.astype(F32)).astype(BF16)


def kernel(
    meta,
    coords,
    weights,
    slave_hbm,
    master_hbm,
    out_master,
    out_slave,
    window,
    slave,
    mortar,
    dual,
    tables,
    first_sq,
    second_sq,
    run,
    mult,
    send_p,
    recv_p,
    send_o,
    recv_o,
    send_h,
    recv_h,
    stage,
    local_sem,
    out_sem,
    halo_h_send,
    halo_h_recv,
    halo_l_send,
    halo_l_recv,
    halo_f_send,
    halo_f_recv,
    force_l_send,
    force_l_recv,
    force_m_send,
    force_m_recv,
    force_h_send,
    force_h_recv,
):
    at_len = lax.axis_index("len")
    at_hgt = lax.axis_index("hgt")
    n_len = lax.axis_size("len")
    n_hgt = lax.axis_size("hgt")
    odd = lax.rem(at_len, 2)
    partner = (at_len + 1 - 2 * odd, at_hgt)
    other = (lax.rem(at_len - 1 + 2 * odd + n_len, n_len), at_hgt)
    above = (at_len, lax.rem(at_hgt + 1, n_hgt))
    below = (at_len, lax.rem(at_hgt + n_hgt - 1, n_hgt))

    def remote(src, dst, send_sem, recv_sem, device):
        return pltpu.make_async_remote_copy(
            src_ref=src,
            dst_ref=dst,
            send_sem=send_sem,
            recv_sem=recv_sem,
            device_id=device,
            device_id_type=MESH,
        )

    def faces(g):
        return pl.ds(g * PART, PART)

    def halo_up(g):
        return remote(
            master_hbm.at[faces(g)],
            window.at[OWN, DOWN, faces(g)],
            halo_h_send.at[0, g],
            halo_h_recv.at[0, g],
            above,
        )

    def halo_down(g):
        return remote(
            master_hbm.at[faces(g)],
            window.at[OWN, UP, faces(g)],
            halo_h_send.at[1, g],
            halo_h_recv.at[1, g],
            below,
        )

    def halo_own(column):
        return remote(
            master_hbm,
            window.at[column, MID],
            halo_l_send.at[column - 1],
            halo_l_recv.at[column - 1],
            partner if column == PARTNER else other,
        )

    def halo_forward(column, row, g):
        return remote(
            window.at[OWN, row, faces(g)],
            window.at[column, row, faces(g)],
            halo_f_send.at[column - 1, row, g],
            halo_f_recv.at[column - 1, row, g],
            partner if column == PARTNER else other,
        )

    def force_len(column, g):
        if column == PARTNER:
            src, dst, device = send_p, recv_p, partner
        else:
            src, dst, device = send_o, recv_o, other
        return remote(
            src.at[g, pl.ds(0, 2)],
            dst.at[g, pl.ds(0, 2)],
            force_l_send.at[column - 1, g],
            force_l_recv.at[column - 1, g],
            device,
        )

    def force_mid(column, g):
        if column == PARTNER:
            src, dst, device = send_p, recv_p, partner
        else:
            src, dst, device = send_o, recv_o, other
        return remote(
            src.at[g, MID],
            dst.at[g, MID],
            force_m_send.at[column - 1, g],
            force_m_recv.at[column - 1, g],
            device,
        )

    def force_hgt(row, g):
        return remote(
            send_h.at[row, g],
            recv_h.at[1 - row, g],
            force_h_send.at[row, g],
            force_h_recv.at[1 - row, g],
            below if row == DOWN else above,
        )

    barrier = pltpu.get_barrier_semaphore()
    for device in (partner, other, above, below):
        pl.semaphore_signal(barrier, inc=1, device_id=device, device_id_type=MESH)
    pl.semaphore_wait(barrier, 4)

    for column in (OTHER, PARTNER):
        halo_own(column).start()
    for g in range(CHUNKS):
        halo_up(g).start()
        halo_down(g).start()
    own_copy = pltpu.make_async_copy(master_hbm, window.at[OWN, MID], local_sem.at[0])
    own_copy.start()
    slave_copy = pltpu.make_async_copy(slave_hbm, slave, local_sem.at[1])
    slave_copy.start()

    modes = lax.broadcasted_iota(jnp.int32, (ORDER, NODES), 0).astype(F32)
    row_ids = lax.broadcasted_iota(jnp.int32, (NODES, NODES), 0)
    col_ids = lax.broadcasted_iota(jnp.int32, (NODES, NODES), 1)

    def build_tables(first_pair):
        def one(i, _):
            points = coords[first_pair + i]
            weight = weights[pl.ds(first_pair + i, 1), :]
            sx, sy, mx, my = (cos_pi(modes * points[k : k + 1]) for k in range(4))
            rows = pl.ds(pl.multiple_of(i * ORDER, ORDER), ORDER)
            tables[i, 0] = sx
            tables[i, 1] = sy
            tables[i, 2] = mx * weight
            tables[i, 3] = my
            first_sq[rows, :] = sx * sx * weight
            second_sq[rows, :] = sy * sy
            return 0

        lax.fori_loop(0, GROUP, one, 0)
        sums = lax.dot_general(
            first_sq[...],
            second_sq[...],
            NT,
            precision=lax.Precision.HIGHEST,
            preferred_element_type=F32,
        )
        sums = jnp.where(row_ids // ORDER == col_ids // ORDER, sums, 0.0)
        spread = jnp.where(row_ids % ORDER == col_ids % ORDER, 1.0, 0.0).astype(F32)
        wide = lax.dot_general(
            sums, spread, NN, precision=lax.Precision.HIGHEST, preferred_element_type=F32
        )
        wide = jnp.where(row_ids % ORDER == col_ids // ORDER, wide, 0.0)
        at = pl.ds(pl.multiple_of(first_pair, GROUP), GROUP)
        dual[at, :] = jnp.sum(wide.reshape(GROUP, ORDER, NODES), axis=1)

    def table_of(i, k):
        first, second = tables[i, k], tables[i, k + 1]
        return (first[:, None, :] * second[None, :, :]).reshape(NODES, NODES)

    def build_mortar(first_pair):
        def some(step, _):
            for u in range(LOCK_A):
                i = step * LOCK_A + u
                slave_high, slave_low = split(table_of(i, 0))
                master_high, master_low = split(table_of(i, 2))
                left = jnp.concatenate([slave_high, slave_low, slave_high], axis=1)
                right = jnp.concatenate([master_high, master_high, master_low], axis=1)
                product = lax.dot_general(left, right, NT, preferred_element_type=F32)
                mortar[first_pair + i] = product.astype(BF16)
            return 0

        lax.fori_loop(0, GROUP // LOCK_A, some, 0)

    def prepare(g, _):
        build_tables(g * GROUP)
        build_mortar(g * GROUP)
        halo_up(g).wait_recv()
        halo_down(g).wait_recv()
        for row in (DOWN, UP):
            for column in (OTHER, PARTNER):
                halo_forward(column, row, g).start()
        return 0

    lax.fori_loop(0, CHUNKS, prepare, 0)

    own_copy.wait()
    slave_copy.wait()
    for column in (PARTNER, OTHER):
        halo_own(column).wait_recv()

    def arrived(g, _):
        for row in (DOWN, UP):
            for column in (PARTNER, OTHER):
                halo_forward(column, row, g).wait_recv()
        return 0

    lax.fori_loop(0, CHUNKS, arrived, 0)

    def contact(step, _):
        slots = [step * LOCK_B + u for u in range(LOCK_B)]
        pairs = [meta[AT_PAIR + t] for t in slots]
        mortars = [mortar[p] for p in pairs]
        projected = []
        for t, matrix in zip(slots, mortars):
            spot = meta[AT_MASTER + t]
            block = spot // FACES
            master = window[block // 3, block % 3, spot % FACES]
            projected.append(lax.dot_general(master, matrix, NT, preferred_element_type=F32))
        multipliers = []
        for t, p, part in zip(slots, pairs, projected):
            diag = dual[pl.ds(p, 1), :]
            gap = slave[meta[AT_SLAVE + t]].astype(F32) * diag - part
            multipliers.append(jnp.where(meta[AT_LIVE + t] > 0, gap * (1.0 / diag), 0.0))
        pushes = [
            jnp.dot(m.astype(BF16), matrix, preferred_element_type=F32)
            for m, matrix in zip(multipliers, mortars)
        ]
        for t, m in zip(slots, multipliers):
            mult[t] = m
        total = run[jnp.maximum(slots[0] - 1, 0)]
        for t, push in zip(slots, pushes):
            total = jnp.where(meta[AT_KEEP + t] > 0, total, 0.0) + push
            run[t] = total
        return 0

    run[0] = jnp.zeros((CHANNELS, NODES), F32)
    lax.fori_loop(0, PAIRS // LOCK_B, contact, 0)

    def force(column, row, face):
        spot = (column * 3 + row) * FACES + face
        return jnp.where(meta[AT_HAS + spot] > 0, run[meta[AT_LAST + spot]], 0.0)

    def fill(g, rows):
        def one(i, _):
            for row in rows:
                send_p[g, row, i] = force(PARTNER, row, g * PART + i)
                send_o[g, row, i] = force(OTHER, row, g * PART + i).astype(BF16)
            return 0

        lax.fori_loop(0, PART, one, 0)

    def send_sides(g, _):
        fill(g, (DOWN, UP))
        for column in (OTHER, PARTNER):
            force_len(column, g).start()
        return 0

    def send_middle(g, _):
        fill(g, (MID,))
        for column in (OTHER, PARTNER):
            force_mid(column, g).start()
        return 0

    lax.fori_loop(0, CHUNKS, send_sides, 0)
    lax.fori_loop(0, CHUNKS, send_middle, 0)

    def add_slaves(face, _):
        def some(step, total):
            for u in range(LOCK_B):
                t = step * LOCK_B + u
                total = total + jnp.where(meta[AT_SLAVE + t] == face, mult[t], 0.0)
            return total

        start = jnp.zeros((CHANNELS, NODES), F32)
        out_slave[face] = lax.fori_loop(0, PAIRS // LOCK_B, some, start)
        return 0

    def send_heights(g, _):
        lax.fori_loop(g * PART, (g + 1) * PART, add_slaves, 0)
        for column in (PARTNER, OTHER):
            force_len(column, g).wait_recv()

        for i in range(PART):
            for row in (DOWN, UP):
                total = force(OWN, row, g * PART + i)
                total = total + recv_p[g, row, i] + recv_o[g, row, i].astype(F32)
                high = total.astype(BF16)
                send_h[row, g, i] = high
                if i < EXTRA:
                    send_h[row, g, PART + i] = (total - high.astype(F32)).astype(BF16)
        for row in (DOWN, UP):
            force_hgt(row, g).start()
        return 0

    lax.fori_loop(0, CHUNKS, send_heights, 0)

    def out_copy(g):
        return pltpu.make_async_copy(stage.at[faces(g)], out_master.at[faces(g)], out_sem.at[g])

    def finish(g, _):
        for column in (PARTNER, OTHER):
            force_mid(column, g).wait_recv()
        for row in (DOWN, UP):
            force_hgt(row, g).wait_recv()
        for i in range(PART):
            total = force(OWN, MID, g * PART + i)
            total = total + recv_p[g, MID, i] + recv_o[g, MID, i].astype(F32)
            for row in (DOWN, UP):
                total = total + recv_h[row, g, i].astype(F32)
                if i < EXTRA:
                    total = total + recv_h[row, g, PART + i].astype(F32)
            stage[g * PART + i] = total
        out_copy(g).start()
        return 0

    lax.fori_loop(0, CHUNKS, finish, 0)

    for column in (PARTNER, OTHER):
        halo_own(column).wait_send()

    def sent(g, _):
        halo_up(g).wait_send()
        halo_down(g).wait_send()
        for column in (PARTNER, OTHER):
            for row in (DOWN, UP):
                halo_forward(column, row, g).wait_send()
            force_len(column, g).wait_send()
            force_mid(column, g).wait_send()
        for row in (DOWN, UP):
            force_hgt(row, g).wait_send()
        out_copy(g).wait()
        return 0

    lax.fori_loop(0, CHUNKS, sent, 0)


def order_pairs(pair_count, slave_face, master_row, master_col, active):
    side = 4
    band_len, band_hgt = lax.axis_index("len"), lax.axis_index("hgt")
    slots = jnp.arange(PAIRS, dtype=jnp.int32)
    live = (slots < pair_count) & (active == 1)
    step_len = master_row // side - band_len
    step_hgt = master_col // side - band_hgt
    column = jnp.where(step_len == 0, OWN, jnp.where(step_len == 1 - 2 * (band_len % 2), PARTNER, OTHER))
    row = jnp.where(step_hgt == 0, MID, jnp.where(step_hgt < 0, DOWN, UP))
    spot = (column * 3 + row) * FACES + (master_row % side) * side + master_col % side
    key = jnp.where(live, spot, SPOTS)
    before = (key[None, :] < key[:, None]) | ((key[None, :] == key[:, None]) & (slots[None, :] < slots[:, None]))
    rank = jnp.sum(before.astype(jnp.int32), axis=1)
    chosen = rank[None, :] == slots[:, None]

    def pick(values):
        return jnp.sum(jnp.where(chosen, values[None, :], 0), axis=1)

    sorted_key = pick(key)
    keep = jnp.concatenate([jnp.zeros((1,), bool), sorted_key[1:] == sorted_key[:-1]])
    spots = jnp.arange(SPOTS, dtype=jnp.int32)
    has = jnp.sum((key[None, :] == spots[:, None]).astype(jnp.int32), axis=1)
    last = jnp.sum((key[None, :] <= spots[:, None]).astype(jnp.int32), axis=1) - 1
    return jnp.concatenate(
        [
            pick(slots),
            jnp.where(sorted_key < SPOTS, sorted_key, 0),
            pick(slave_face),
            (sorted_key < SPOTS).astype(jnp.int32),
            keep.astype(jnp.int32),
            jnp.maximum(last, 0),
            has,
        ]
    )


def body(
    slave_disp,
    master_disp,
    quad_coords,
    quad_weights,
    pair_count,
    slave_face,
    master_row,
    master_col,
    active,
):
    meta = order_pairs(
        pair_count[0, 0], slave_face[0, 0], master_row[0, 0], master_col[0, 0], active[0, 0]
    )
    face = (CHANNELS, NODES)
    dma = pltpu.SemaphoreType.DMA
    out = jax.ShapeDtypeStruct((FACES, *face), F32)
    vmem = pl.BlockSpec(memory_space=pltpu.VMEM)
    hbm = pl.BlockSpec(memory_space=pl.ANY)
    master_force, slave_sum = pl.pallas_call(
        kernel,
        out_shape=(out, out),
        in_specs=[pl.BlockSpec(memory_space=pltpu.SMEM), vmem, vmem, hbm, hbm],
        out_specs=(hbm, vmem),
        scratch_shapes=[
            pltpu.VMEM((3, 3, FACES, *face), BF16),
            pltpu.VMEM((FACES, *face), BF16),
            pltpu.VMEM((PAIRS, NODES, NODES), BF16),
            pltpu.VMEM((PAIRS, NODES), F32),
            pltpu.VMEM((GROUP, 4, ORDER, NODES), F32),
            pltpu.VMEM((NODES, NODES), F32),
            pltpu.VMEM((NODES, NODES), F32),
            pltpu.VMEM((PAIRS, *face), F32),
            pltpu.VMEM((PAIRS, *face), F32),
            pltpu.VMEM((CHUNKS, 3, PART, *face), F32),
            pltpu.VMEM((CHUNKS, 3, PART, *face), F32),
            pltpu.VMEM((CHUNKS, 3, PART, *face), BF16),
            pltpu.VMEM((CHUNKS, 3, PART, *face), BF16),
            pltpu.VMEM((2, CHUNKS, PART + EXTRA, *face), BF16),
            pltpu.VMEM((2, CHUNKS, PART + EXTRA, *face), BF16),
            pltpu.VMEM((FACES, *face), F32),
            dma((2,)),
            dma((CHUNKS,)),
            dma((2, CHUNKS)),
            dma((2, CHUNKS)),
            dma((2,)),
            dma((2,)),
            dma((2, 2, CHUNKS)),
            dma((2, 2, CHUNKS)),
            dma((2, CHUNKS)),
            dma((2, CHUNKS)),
            dma((2, CHUNKS)),
            dma((2, CHUNKS)),
            dma((2, CHUNKS)),
            dma((2, CHUNKS)),
        ],
        compiler_params=pltpu.CompilerParams(
            collective_id=0, has_side_effects=True, vmem_limit_bytes=60 * 2**20
        ),
    )(
        meta,
        quad_coords.reshape(PAIRS, 4, NODES),
        quad_weights.reshape(PAIRS, NODES),
        slave_disp.reshape(FACES, *face),
        master_disp.reshape(FACES, *face),
    )
    return (
        master_force.reshape(4, 4, *face),
        slave_sum.reshape(4, 4, *face),
    )


def solution(mesh):
    in_specs = (
        P("len", "hgt", None, None),
        P("len", "hgt", None, None),
        P("len", "hgt", None, None, None),
        P("len", "hgt", None, None),
        P("len", "hgt"),
        P("len", "hgt", None),
        P("len", "hgt", None),
        P("len", "hgt", None),
        P("len", "hgt", None),
    )
    out_specs = (P("len", "hgt", None, None), P("len", "hgt", None, None))
    return jax.shard_map(body, mesh=mesh, in_specs=in_specs, out_specs=out_specs, check_vma=False)
```

time: 313 us -> 83.1 us (0.27)
  the two profiles are of different devices: /device:TPU:111 before, /device:TPU:24 now
where the time goes in v1:
time: 83.1 us; the launch traced here: 82.9 us
  Pallas kernels  75 us (90%)
  local copies, waits for them, and re-layouts  4.63 us (6%)
  other arithmetic  1.96 us (2%)
  between operations  1.31 us (2%)
    pallas_call x1, Pallas kernels, body(): pl.pallas_call(kernel, out_shape=(out, out), in_specs=[pl.BlockSpec(memor...  75 us
    unnamed x4, local copies, waits for them, and re-layouts  3.95 us

profile of v1, /device:TPU:24, one launch (start us, length us, event | category | flops | bytes accessed | tf_op | source)
XLA Modules:
  0.0 82.9 jit_solution(16081391211423874807)
XLA Ops:
  1.3 0.7 fusion.2
  2.0 0.2 convert_reduce_fusion.2
  2.2 0.8 select_reduce_fusion
  3.0 0.1 slice_compare_fusion
  3.1 0.1 compare_convert_fusion
  3.1 0.1 convert_reduce_fusion
  3.3 0.7 concatenate.7.meta
  3.9 75.0 %shard_map.104 = (f32[16,96,256]{2,1,0:T(8,128)}, f32[16,96,256]{2,1,0:T(8,128)}) custom-call(s32[608]{0:T(1024)} %concatenate.7.meta, f32[64,4,256]{2,1,0:T(4,128)} %bitcast.43, f32[64,256]{1,0:T(8,128)} %bitcast.44, bf16[16,96,256]{2,1,0:T(8,128)(2,1)} %bitcast.41, bf16[16,96,256]{2,1,0:T(8,128)(2,1)} %bitcast.42), custom_call_target="tpu_custom_call" | custom-call | tf_op jit(solution)/shard_map/pallas_call | solution.py:460
  79.0 0.0 copy-start
  79.0 2.8 %copy.14 = f32[4,4,96,256]{3,2,1,0:T(8,128)} copy(f32[4,4,96,256]{3,2,1,0:T(8,128)} %bitcast.40) | data formatting | bytes 3145728
  81.8 0.0 copy-done
  81.8 1.1 %copy.15 = f32[4,4,96,256]{3,2,1,0:T(8,128)} copy(f32[4,4,96,256]{3,2,1,0:T(8,128)S(1)} %bitcast.39) | data formatting | bytes 3145728
  (2 shorter events, 0.0 us)
Async XLA Ops:
  79.0 2.8 %copy-start = (f32[16,96,256]{2,1,0:T(8,128)S(1)}, f32[16,96,256]{2,1,0:T(8,128)}, u32[]{:S(2)}) copy-start(f32[16,96,256]{2,1,0:T(8,128)} %get-tuple-element.5) | copy-start | bytes 4718596

commit v2 on v1

v2 whole, which is shorter than its diff:
```python
import functools

import jax
import jax.numpy as jnp
from jax import lax
from jax.experimental import pallas as pl
from jax.experimental.pallas import tpu as pltpu
from jax.sharding import PartitionSpec as P

ORDER = 16
NODES = 256
CHANNELS = 96
FACES = 16
PAIRS = 64
GROUP = 16
LOCK_A = 4
LOCK_B = 8
CHUNKS = 4
PART = FACES // CHUNKS
F32, BF16 = jnp.float32, jnp.bfloat16
MESH = pl.DeviceIdType.MESH
NT = (((1,), (1,)), ((), ()))
NN = (((1,), (0,)), ((), ()))

OWN, PARTNER, OTHER = range(3)
DOWN, UP, MID = range(3)
BLOCKS = 9
SPOTS = BLOCKS * FACES

AT_PAIR, AT_MASTER, AT_SLAVE, AT_LAST = range(4)
META = (8, 256)
TURN = CHUNKS - 1


def cos_pi(turns):
    reduced = turns - 2.0 * jnp.round(turns * 0.5)
    s = (0.5 - jnp.abs(reduced)) - 1.4e-8
    s2 = s * s
    p = jnp.float32(-0.00737043)
    for c in (0.082145887, -0.59926453, 2.5501640, -5.1677128, 3.1415927):
        p = p * s2 + jnp.float32(c)
    return p * s


def split(value):
    high = value.astype(BF16)
    return high, (value - high.astype(F32)).astype(BF16)


def order_pairs(pair_count, ints, order):
    side = 4
    at_len, at_hgt = lax.axis_index("len"), lax.axis_index("hgt")
    square = (PAIRS, PAIRS)
    down, along = (lax.broadcasted_iota(jnp.int32, square, d) for d in (0, 1))
    slots = lax.broadcasted_iota(jnp.int32, (1, PAIRS), 1)
    slave_face, master_row, master_col, active = (ref[...] for ref in ints)
    live = (slots < pair_count[0, 0]) & (active == 1)
    step_len = master_row // side - at_len
    step_hgt = master_col // side - at_hgt
    column = jnp.where(step_len == 0, OWN, jnp.where(step_len == 1 - 2 * lax.rem(at_len, 2), PARTNER, OTHER))
    row = jnp.where(step_hgt == 0, MID, jnp.where(step_hgt < 0, DOWN, UP))
    spot = (column * 3 + row) * FACES + (master_row % side) * side + master_col % side
    key = jnp.where(live, spot, SPOTS)

    def stand(values):
        return jnp.sum(jnp.where(down == along, values, 0), axis=1, keepdims=True)

    key_col = stand(key)
    before = (key < key_col) | ((key == key_col) & (along < down))
    rank = jnp.sum(before.astype(jnp.int32), axis=1, keepdims=True)
    chosen = rank == along

    def pick(values):
        return jnp.sum(jnp.where(chosen, values, 0), axis=0, keepdims=True)

    spots = lax.broadcasted_iota(jnp.int32, (PAIRS, META[1]), 1)
    has = jnp.sum((key_col == spots).astype(jnp.int32), axis=0, keepdims=True)
    upto = jnp.sum((key_col <= spots).astype(jnp.int32), axis=0, keepdims=True)
    order[...] = jnp.zeros(META, jnp.int32)
    order[AT_PAIR : AT_PAIR + 1, :PAIRS] = pick(down)
    order[AT_MASTER : AT_MASTER + 1, :PAIRS] = pick(key_col)
    order[AT_SLAVE : AT_SLAVE + 1, :PAIRS] = pick(stand(slave_face))
    order[AT_LAST : AT_LAST + 1, :] = jnp.where(has > 0, upto - 1, -1)


def kernel(
    pair_count,
    slave_face,
    master_row,
    master_col,
    active,
    coords,
    weights,
    slave_hbm,
    master_hbm,
    out_master,
    out_slave,
    order,
    meta,
    points,
    point_weights,
    window,
    slave,
    mortar,
    dual,
    tables,
    first_sq,
    second_sq,
    run,
    mult,
    send_p,
    recv_p,
    send_o,
    recv_o,
    recv_d,
    send_h,
    recv_h,
    local_sem,
    halo_h_send,
    halo_h_recv,
    halo_p_send,
    halo_p_recv,
    halo_o_send,
    halo_o_recv,
    halo_d_send,
    halo_d_recv,
    halo_f_send,
    halo_f_recv,
    force_l_send,
    force_l_recv,
    force_m_send,
    force_m_recv,
    force_d_send,
    force_d_recv,
    force_h_send,
    force_h_recv,
):
    at_len = lax.axis_index("len")
    at_hgt = lax.axis_index("hgt")
    n_len = lax.axis_size("len")
    n_hgt = lax.axis_size("hgt")
    odd = lax.rem(at_len, 2)
    other_len = at_len - 1 + 2 * odd
    partner = (at_len + 1 - 2 * odd, at_hgt)
    other = (lax.rem(other_len + n_len, n_len), at_hgt)
    above = (at_len, lax.rem(at_hgt + 1, n_hgt))
    below = (at_len, lax.rem(at_hgt + n_hgt - 1, n_hgt))
    has_other = (other_len >= 0) & (other_len < n_len)
    has_row = (at_hgt > 0, at_hgt < n_hgt - 1)
    beside = (below, above)
    neighbours = ((partner, None), (other, has_other), (below, has_row[DOWN]), (above, has_row[UP]))

    def when(condition, action):
        if condition is None:
            action()
        else:
            pl.when(condition)(action)

    def both(first, second):
        return second if first is None else first & second

    def remote(src, dst, send_sem, recv_sem, device):
        return pltpu.make_async_remote_copy(
            src_ref=src,
            dst_ref=dst,
            send_sem=send_sem,
            recv_sem=recv_sem,
            device_id=device,
            device_id_type=MESH,
        )

    def faces(g):
        return pl.ds(g * PART, PART)

    def halo_hgt(row, g):
        return remote(
            master_hbm.at[faces(g)],
            window.at[OWN, 1 - row, faces(g)],
            halo_h_send.at[row, g],
            halo_h_recv.at[1 - row, g],
            beside[row],
        )

    def halo_partner():
        return remote(
            master_hbm, window.at[PARTNER, MID], halo_p_send.at[0], halo_p_recv.at[0], partner
        )

    def halo_other(g):
        return remote(
            master_hbm.at[faces(g)],
            window.at[OTHER, MID, faces(g)],
            halo_o_send.at[g],
            halo_o_recv.at[g],
            other,
        )

    def halo_turn(row):
        return remote(
            window.at[OTHER, MID, faces(TURN)],
            window.at[OTHER, 1 - row, faces(TURN)],
            halo_d_send.at[row],
            halo_d_recv.at[1 - row],
            beside[row],
        )

    def halo_forward(column, row, g):
        return remote(
            window.at[OWN, row, faces(g)],
            window.at[column, row, faces(g)],
            halo_f_send.at[column - 1, row, g],
            halo_f_recv.at[column - 1, row, g],
            partner if column == PARTNER else other,
        )

    def force_len(column, g):
        if column == PARTNER:
            src, dst, device = send_p, recv_p, partner
        else:
            src, dst, device = send_o, recv_o, other
        return remote(
            src.at[g, pl.ds(0, 2)],
            dst.at[g, pl.ds(0, 2)],
            force_l_send.at[column - 1, g],
            force_l_recv.at[column - 1, g],
            device,
        )

    def force_mid(column, g):
        if column == PARTNER:
            src, dst, device = send_p, recv_p, partner
        else:
            src, dst, device = send_o, recv_o, other
        return remote(
            src.at[g, MID],
            dst.at[g, MID],
            force_m_send.at[column - 1, g],
            force_m_recv.at[column - 1, g],
            device,
        )

    def force_turn(row):
        return remote(
            send_o.at[TURN, row],
            recv_d.at[1 - row],
            force_d_send.at[row],
            force_d_recv.at[1 - row],
            beside[row],
        )

    def force_hgt(row, g):
        return remote(
            send_h.at[row, g],
            recv_h.at[1 - row, g],
            force_h_send.at[row, g],
            force_h_recv.at[1 - row, g],
            beside[row],
        )

    barrier = pltpu.get_barrier_semaphore()
    for device, there in neighbours:

        def greet(device=device):
            pl.semaphore_signal(barrier, inc=1, device_id=device, device_id_type=MESH)

        when(there, greet)
    loads = [
        pltpu.make_async_copy(coords, points, local_sem.at[0]),
        pltpu.make_async_copy(weights, point_weights, local_sem.at[1]),
        pltpu.make_async_copy(master_hbm, window.at[OWN, MID], local_sem.at[2]),
        pltpu.make_async_copy(slave_hbm, slave, local_sem.at[3]),
    ]
    for load in loads:
        load.start()
    pl.semaphore_wait(barrier, 1 + sum(there.astype(jnp.int32) for _, there in neighbours[1:]))

    @pl.when(has_other)
    def _():
        for g in (TURN, *range(TURN)):
            halo_other(g).start()

    halo_partner().start()
    for g in range(CHUNKS):
        for row in (DOWN, UP):
            when(has_row[row], lambda row=row, g=g: halo_hgt(row, g).start())

    order_pairs(pair_count, (slave_face, master_row, master_col, active), order)
    publish = pltpu.make_async_copy(order, meta, local_sem.at[4])
    publish.start()
    loads[0].wait()
    loads[1].wait()

    modes = lax.broadcasted_iota(jnp.int32, (ORDER, NODES), 0).astype(F32)
    row_ids = lax.broadcasted_iota(jnp.int32, (NODES, NODES), 0)
    col_ids = lax.broadcasted_iota(jnp.int32, (NODES, NODES), 1)

    def build_tables(first_pair):
        def one(i, _):
            place = points[first_pair + i]
            weight = point_weights[pl.ds(first_pair + i, 1), :]
            sx, sy, mx, my = (cos_pi(modes * place[k : k + 1]) for k in range(4))
            rows = pl.ds(pl.multiple_of(i * ORDER, ORDER), ORDER)
            tables[i, 0] = sx
            tables[i, 1] = sy
            tables[i, 2] = mx * weight
            tables[i, 3] = my
            first_sq[rows, :] = sx * sx * weight
            second_sq[rows, :] = sy * sy
            return 0

        lax.fori_loop(0, GROUP, one, 0)
        sums = lax.dot_general(
            first_sq[...],
            second_sq[...],
            NT,
            precision=lax.Precision.HIGHEST,
            preferred_element_type=F32,
        )
        sums = jnp.where(row_ids // ORDER == col_ids // ORDER, sums, 0.0)
        spread = jnp.where(row_ids % ORDER == col_ids % ORDER, 1.0, 0.0).astype(F32)
        wide = lax.dot_general(
            sums, spread, NN, precision=lax.Precision.HIGHEST, preferred_element_type=F32
        )
        wide = jnp.where(row_ids % ORDER == col_ids // ORDER, wide, 0.0)
        at = pl.ds(pl.multiple_of(first_pair, GROUP), GROUP)
        dual[at, :] = jnp.sum(wide.reshape(GROUP, ORDER, NODES), axis=1)

    def table_of(i, k):
        first, second = tables[i, k], tables[i, k + 1]
        return (first[:, None, :] * second[None, :, :]).reshape(NODES, NODES)

    def build_mortar(first_pair):
        def some(step, _):
            for u in range(LOCK_A):
                i = step * LOCK_A + u
                slave_high, slave_low = split(table_of(i, 0))
                master_high, master_low = split(table_of(i, 2))
                left = jnp.concatenate([slave_high, slave_low, slave_high], axis=1)
                right = jnp.concatenate([master_high, master_high, master_low], axis=1)
                product = lax.dot_general(left, right, NT, preferred_element_type=F32)
                mortar[first_pair + i] = product.astype(BF16)
            return 0

        lax.fori_loop(0, GROUP // LOCK_A, some, 0)

    def prepare(g, _):
        build_tables(g * GROUP)
        build_mortar(g * GROUP)

        @pl.when((g == 0) & has_other)
        def _():
            halo_other(TURN).wait_recv()
            for row in (DOWN, UP):
                when(has_row[row], lambda row=row: halo_turn(row).start())

        for row in (DOWN, UP):

            def pass_on(row=row):
                halo_hgt(1 - row, g).wait_recv()
                pl.when(has_other & (g != TURN))(lambda: halo_forward(OTHER, row, g).start())
                halo_forward(PARTNER, row, g).start()

            when(has_row[row], pass_on)
        return 0

    lax.fori_loop(0, CHUNKS, prepare, 0)

    publish.wait()
    loads[2].wait()
    loads[3].wait()
    halo_partner().wait_recv()

    def arrived(g, _):
        pl.when(has_other)(lambda: halo_other_rest(g))
        for row in (DOWN, UP):

            def rest(row=row):
                halo_forward(PARTNER, row, g).wait_recv()
                pl.when(has_other & (g != TURN))(lambda: halo_forward(OTHER, row, g).wait_recv())
                pl.when(has_other & (g == TURN))(lambda: halo_turn(1 - row).wait_recv())

            when(has_row[row], rest)
        return 0

    def halo_other_rest(g):
        pl.when(g != TURN)(lambda: halo_other(g).wait_recv())

    lax.fori_loop(0, CHUNKS, arrived, 0)

    @pl.when(jnp.logical_not(has_other))
    def _():
        recv_o[...] = jnp.zeros(recv_o.shape, BF16)

    for row in (DOWN, UP):

        @pl.when(jnp.logical_not(has_row[row]))
        def _(row=row):
            recv_h[row] = jnp.zeros(recv_h.shape[1:], BF16)
            recv_d[row] = jnp.zeros(recv_d.shape[1:], BF16)

    def contact(step, _):
        slots = [step * LOCK_B + u for u in range(LOCK_B)]
        pairs = [meta[AT_PAIR, t] for t in slots]
        keys = [meta[AT_MASTER, t] for t in slots]
        mortars = [mortar[p] for p in pairs]
        projected = []
        for key, matrix in zip(keys, mortars):
            spot = jnp.where(key < SPOTS, key, MID * FACES)
            block = spot // FACES
            master = window[block // 3, block % 3, spot % FACES]
            projected.append(lax.dot_general(master, matrix, NT, preferred_element_type=F32))
        multipliers = []
        for t, p, key, part in zip(slots, pairs, keys, projected):
            diag = dual[pl.ds(p, 1), :]
            gap = slave[meta[AT_SLAVE, t]].astype(F32) * diag - part
            multipliers.append(jnp.where(key < SPOTS, gap * (1.0 / diag), 0.0))
        pushes = [
            jnp.dot(m.astype(BF16), matrix, preferred_element_type=F32)
            for m, matrix in zip(multipliers, mortars)
        ]
        for t, m in zip(slots, multipliers):
            mult[t] = m
        total = run[jnp.maximum(slots[0] - 1, 0)]
        last = meta[AT_MASTER, jnp.maximum(slots[0] - 1, 0)]
        for t, key, push in zip(slots, keys, pushes):
            total = jnp.where(key == last, total, 0.0) + push
            run[t] = total
            last = key
        return 0

    run[0] = jnp.zeros((CHANNELS, NODES), F32)
    lax.fori_loop(0, PAIRS // LOCK_B, contact, 0)

    def force(column, row, face):
        last = meta[AT_LAST, (column * 3 + row) * FACES + face]
        return jnp.where(last >= 0, run[jnp.maximum(last, 0)], 0.0)

    def fill(column, g, rows):
        send = send_p if column == PARTNER else send_o

        def one(i, _):
            for row in rows:
                send[g, row, i] = force(column, row, g * PART + i).astype(send.dtype)
            return 0

        lax.fori_loop(0, PART, one, 0)

    def to_other(action):
        pl.when(has_other)(action)

    fill(OTHER, TURN, (DOWN, UP))
    for row in (DOWN, UP):
        when(has_row[row], lambda row=row: force_turn(row).start())

    def send_sides(g, _):
        fill(OTHER, g, (DOWN, UP))
        to_other(lambda: force_len(OTHER, g).start())
        return 0

    def send_partner(k, _):
        g = lax.rem(k + TURN, CHUNKS)
        fill(PARTNER, g, (DOWN, UP))
        force_len(PARTNER, g).start()
        return 0

    def send_middle(g, _):
        fill(OTHER, g, (MID,))
        to_other(lambda: force_mid(OTHER, g).start())
        return 0

    def send_partner_middle(g, _):
        fill(PARTNER, g, (MID,))
        force_mid(PARTNER, g).start()
        return 0

    lax.fori_loop(0, 1, send_sides, 0)
    lax.fori_loop(0, 1, send_partner, 0)
    lax.fori_loop(1, TURN, send_sides, 0)
    lax.fori_loop(1, CHUNKS, send_partner, 0)
    lax.fori_loop(0, TURN, send_middle, 0)
    lax.fori_loop(0, CHUNKS, send_partner_middle, 0)

    def add_slaves(face, _):
        def some(step, total):
            for u in range(LOCK_B):
                t = step * LOCK_B + u
                total = total + jnp.where(meta[AT_SLAVE, t] == face, mult[t], 0.0)
            return total

        start = jnp.zeros((CHANNELS, NODES), F32)
        out_slave[face] = lax.fori_loop(0, PAIRS // LOCK_B, some, start)
        return 0

    def send_heights(k, _):
        g = lax.rem(k + TURN, CHUNKS)
        force_len(PARTNER, g).wait_recv()
        for row in (DOWN, UP):
            for i in range(PART):
                total = force(OWN, row, g * PART + i) + recv_p[g, row, i]
                send_h[row, g, i] = total.astype(BF16)

        @pl.when(g != TURN)
        def _():
            to_other(lambda: force_len(OTHER, g).wait_recv())
            for row in (DOWN, UP):
                for i in range(PART):
                    total = force(OWN, row, g * PART + i) + recv_p[g, row, i]
                    send_h[row, g, i] = (total + recv_o[g, row, i].astype(F32)).astype(BF16)

        for row in (DOWN, UP):
            when(has_row[row], lambda row=row: force_hgt(row, g).start())

        @pl.when(g == TURN)
        def _():
            for row in (DOWN, UP):
                when(has_row[row], lambda row=row: force_turn(1 - row).wait_recv())
            for i in range(PART):
                total = force(OTHER, MID, g * PART + i)
                for row in (DOWN, UP):
                    total = total + recv_d[row, i].astype(F32)
                send_o[g, MID, i] = total.astype(BF16)
            to_other(lambda: force_mid(OTHER, g).start())

        lax.fori_loop(k * PART, (k + 1) * PART, add_slaves, 0)
        return 0

    lax.fori_loop(0, CHUNKS, send_heights, 0)

    def finish(g, _):
        force_mid(PARTNER, g).wait_recv()
        to_other(lambda: force_mid(OTHER, g).wait_recv())
        for row in (DOWN, UP):
            when(has_row[row], lambda row=row: force_hgt(1 - row, g).wait_recv())
        for i in range(PART):
            total = force(OWN, MID, g * PART + i)
            total = total + recv_p[g, MID, i] + recv_o[g, MID, i].astype(F32)
            for row in (DOWN, UP):
                total = total + recv_h[row, g, i].astype(F32)
            out_master[g * PART + i] = total
        return 0

    lax.fori_loop(0, CHUNKS, finish, 0)

    halo_partner().wait_send()
    for row in (DOWN, UP):
        when(has_row[row], lambda row=row: force_turn(row).wait_send())
        when(has_row[row] & has_other, lambda row=row: halo_turn(row).wait_send())

    def sent(g, _):
        to_other(lambda: halo_other(g).wait_send())
        force_len(PARTNER, g).wait_send()
        force_mid(PARTNER, g).wait_send()
        to_other(lambda: force_mid(OTHER, g).wait_send())
        pl.when(has_other & (g != TURN))(lambda: force_len(OTHER, g).wait_send())
        for row in (DOWN, UP):

            def rest(row=row):
                halo_hgt(row, g).wait_send()
                force_hgt(row, g).wait_send()
                halo_forward(PARTNER, row, g).wait_send()
                pl.when(has_other & (g != TURN))(lambda: halo_forward(OTHER, row, g).wait_send())

            when(has_row[row], rest)
        return 0

    lax.fori_loop(0, CHUNKS, sent, 0)


def store(master_in, slave_in, master_out, slave_out, sem):
    copies = [
        pltpu.make_async_copy(master_in, master_out, sem.at[0]),
        pltpu.make_async_copy(slave_in, slave_out, sem.at[1]),
    ]
    for copy in copies:
        copy.start()
    for copy in copies:
        copy.wait()


def body(
    slave_disp,
    master_disp,
    quad_coords,
    quad_weights,
    pair_count,
    slave_face,
    master_row,
    master_col,
    active,
):
    face = (CHANNELS, NODES)
    dma = pltpu.SemaphoreType.DMA
    out = jax.ShapeDtypeStruct((FACES, *face), F32)
    held = pltpu.VMEM((FACES, *face), F32)
    vmem = pl.BlockSpec(memory_space=pltpu.VMEM)
    hbm = pl.BlockSpec(memory_space=pl.ANY)
    slots = (1, PAIRS)
    results = pl.pallas_call(
        kernel,
        out_shape=(held, held),
        in_specs=[pl.BlockSpec(memory_space=pltpu.SMEM), *[vmem] * 4, *[hbm] * 4],
        out_specs=(vmem, vmem),
        scratch_shapes=[
            pltpu.VMEM(META, jnp.int32),
            pltpu.SMEM(META, jnp.int32),
            pltpu.VMEM((PAIRS, 4, NODES), F32),
            pltpu.VMEM((PAIRS, NODES), F32),
            pltpu.VMEM((3, 3, FACES, *face), BF16),
            pltpu.VMEM((FACES, *face), BF16),
            pltpu.VMEM((PAIRS, NODES, NODES), BF16),
            pltpu.VMEM((PAIRS, NODES), F32),
            pltpu.VMEM((GROUP, 4, ORDER, NODES), F32),
            pltpu.VMEM((NODES, NODES), F32),
            pltpu.VMEM((NODES, NODES), F32),
            pltpu.VMEM((PAIRS, *face), F32),
            pltpu.VMEM((PAIRS, *face), F32),
            pltpu.VMEM((CHUNKS, 3, PART, *face), F32),
            pltpu.VMEM((CHUNKS, 3, PART, *face), F32),
            pltpu.VMEM((CHUNKS, 3, PART, *face), BF16),
            pltpu.VMEM((CHUNKS, 3, PART, *face), BF16),
            pltpu.VMEM((2, PART, *face), BF16),
            pltpu.VMEM((2, CHUNKS, PART, *face), BF16),
            pltpu.VMEM((2, CHUNKS, PART, *face), BF16),
            dma((5,)),
            *[dma((2, CHUNKS))] * 2,
            *[dma((1,))] * 2,
            *[dma((CHUNKS,))] * 2,
            *[dma((2,))] * 2,
            *[dma((2, 2, CHUNKS))] * 2,
            *[dma((2, CHUNKS))] * 2,
            *[dma((2, CHUNKS))] * 2,
            *[dma((2,))] * 2,
            *[dma((2, CHUNKS))] * 2,
        ],
        compiler_params=pltpu.CompilerParams(
            collective_id=0, has_side_effects=True, vmem_limit_bytes=56 * 2**20
        ),
        name="contact",
    )(
        pair_count,
        slave_face.reshape(slots),
        master_row.reshape(slots),
        master_col.reshape(slots),
        active.reshape(slots),
        quad_coords.reshape(PAIRS, 4, NODES),
        quad_weights.reshape(PAIRS, NODES),
        slave_disp.reshape(FACES, *face),
        master_disp.reshape(FACES, *face),
    )
    results = [pltpu.with_memory_space_constraint(r, pltpu.VMEM) for r in results]
    master_force, slave_sum = pl.pallas_call(
        store,
        out_shape=(out, out),
        in_specs=[vmem, vmem],
        out_specs=(hbm, hbm),
        scratch_shapes=[dma((2,))],
        compiler_params=pltpu.CompilerParams(vmem_limit_bytes=2**20),
        name="store",
    )(*results)
    return (
        master_force.reshape(4, 4, *face),
        slave_sum.reshape(4, 4, *face),
    )


def solution(mesh):
    in_specs = (
        P("len", "hgt", None, None),
        P("len", "hgt", None, None),
        P("len", "hgt", None, None, None),
        P("len", "hgt", None, None),
        P("len", "hgt"),
        P("len", "hgt", None),
        P("len", "hgt", None),
        P("len", "hgt", None),
        P("len", "hgt", None),
    )
    out_specs = (P("len", "hgt", None, None), P("len", "hgt", None, None))
    return jax.shard_map(body, mesh=mesh, in_specs=in_specs, out_specs=out_specs, check_vma=False)
```

time: 83.1 us -> 63.8 us (0.77)
  the two profiles are of different devices: /device:TPU:24 before, /device:TPU:111 now
where the time goes in v2:
time: 63.8 us; the launch traced here: 63.7 us
  Pallas kernels  62.4 us (98%)
  between operations  1.29 us (2%)
    pallas_call x1, Pallas kernels, body(): pl.pallas_call(kernel, out_shape=(held, held), in_specs=[pl.BlockSpec(mem...  60.7 us
    pallas_call x1, Pallas kernels, body(): pl.pallas_call(store, out_shape=(out, out), in_specs=[vmem, vmem], out_sp...  1.68 us

profile of v2, /device:TPU:111, one launch (start us, length us, event | category | flops | bytes accessed | tf_op | source)
XLA Modules:
  0.0 63.7 jit_solution(614798056286163911)
XLA Ops:
  1.3 60.7 %contact.1 = (f32[16,96,256]{2,1,0:T(8,128)S(1)}, f32[16,96,256]{2,1,0:T(8,128)S(1)}) custom-call(s32[1,1]{1,0:T(1,128)S(6)} %copy.11.pair_count, s32[1,64]{1,0:T(1,128)} %bitcast.14, s32[1,64]{1,0:T(1,128)} %bitcast.15, s32[1,64]{1,0:T(1,128)} %bitcast.16, s32[1,64]{1,0:T(1,128)} %bitcast.17, f32[64,4,256]{2,1,0:T(4,128)} %bitcast.12, f32[64,256]{1,0:T(8,128)} %bitcast.13, ...), custom_call_target="tpu_custom_call" | custom-call | tf_op jit(solution)/shard_map/contact/pallas_call | solution.py:598
  62.0 1.7 %store.1 = (f32[16,96,256]{2,1,0:T(8,128)}, f32[16,96,256]{2,1,0:T(8,128)}) custom-call(f32[16,96,256]{2,1,0:T(8,128)S(1)} %get-tuple-element.6.master_in, f32[16,96,256]{2,1,0:T(8,128)S(1)} %get-tuple-element.7.slave_in), custom_call_target="tpu_custom_call" | custom-call | tf_op jit(solution)/shard_map/store/pallas_call | solution.py:651

commit v3 on v2

v3 whole, which is shorter than its diff:
```python
import functools

import jax
import jax.numpy as jnp
from jax import lax
from jax.experimental import pallas as pl
from jax.experimental.pallas import tpu as pltpu
from jax.sharding import PartitionSpec as P

ORDER = 16
NODES = 256
CHANNELS = 96
FACES = 16
PAIRS = 64
GROUP = 16
LOCK_A = 8
LOCK_S = 8
LOCK_B = 16
CHUNKS = 4
HALVES = 2
ROWS = CHANNELS // HALVES
PART = FACES // CHUNKS
F32, BF16 = jnp.float32, jnp.bfloat16
MESH = pl.DeviceIdType.MESH
NT = (((1,), (1,)), ((), ()))
NN = (((1,), (0,)), ((), ()))

OWN, PARTNER, OTHER = range(3)
DOWN, UP, MID = range(3)
BLOCKS = 9
SPOTS = BLOCKS * FACES

AT_PAIR, AT_MASTER, AT_SLAVE, AT_LAST = range(4)
AT_TURN, AT_FACE, AT_END = range(4, 7)
META = (8, 256)
TURN = CHUNKS - 1


def cos_pi(turns):
    reduced = turns - 2.0 * jnp.round(turns * 0.5)
    s = (0.5 - jnp.abs(reduced)) - 1.4e-8
    s2 = s * s
    p = jnp.float32(-0.00737043)
    for c in (0.082145887, -0.59926453, 2.5501640, -5.1677128, 3.1415927):
        p = p * s2 + jnp.float32(c)
    return p * s


def split(value):
    high = value.astype(BF16)
    return high, (value - high.astype(F32)).astype(BF16)


def order_pairs(pair_count, ints, order):
    side = 4
    at_len, at_hgt = lax.axis_index("len"), lax.axis_index("hgt")
    square = (PAIRS, PAIRS)
    down, along = (lax.broadcasted_iota(jnp.int32, square, d) for d in (0, 1))
    slots = lax.broadcasted_iota(jnp.int32, (1, PAIRS), 1)
    slave_face, master_row, master_col, active = (ref[...] for ref in ints)
    live = (slots < pair_count[0, 0]) & (active == 1)
    step_len = master_row // side - at_len
    step_hgt = master_col // side - at_hgt
    column = jnp.where(step_len == 0, OWN, jnp.where(step_len == 1 - 2 * lax.rem(at_len, 2), PARTNER, OTHER))
    row = jnp.where(step_hgt == 0, MID, jnp.where(step_hgt < 0, DOWN, UP))
    spot = (column * 3 + row) * FACES + (master_row % side) * side + master_col % side
    key = jnp.where(live, spot, SPOTS)

    def stand(values):
        return jnp.sum(jnp.where(down == along, values, 0), axis=1, keepdims=True)

    def rank_of(key, key_col):
        before = (key < key_col) | ((key == key_col) & (along < down))
        return jnp.sum(before.astype(jnp.int32), axis=1, keepdims=True)

    def pick(rank, values):
        return jnp.sum(jnp.where(rank == along, values, 0), axis=0, keepdims=True)

    spots = lax.broadcasted_iota(jnp.int32, (PAIRS, META[1]), 1)

    def last_of(key_col):
        has = jnp.sum((key_col == spots).astype(jnp.int32), axis=0, keepdims=True)
        upto = jnp.sum((key_col <= spots).astype(jnp.int32), axis=0, keepdims=True)
        return jnp.where(has > 0, upto - 1, -1)

    key_col = stand(key)
    rank = rank_of(key, key_col)
    face_key = jnp.where(live, slave_face, FACES)
    face_col = stand(face_key)
    face_rank = rank_of(face_key, face_col)
    order[...] = jnp.zeros(META, jnp.int32)
    order[AT_PAIR : AT_PAIR + 1, :PAIRS] = pick(rank, down)
    order[AT_MASTER : AT_MASTER + 1, :PAIRS] = pick(rank, key_col)
    order[AT_SLAVE : AT_SLAVE + 1, :PAIRS] = pick(rank, stand(slave_face))
    order[AT_LAST : AT_LAST + 1, :] = last_of(key_col)
    order[AT_TURN : AT_TURN + 1, :PAIRS] = pick(face_rank, rank)
    order[AT_FACE : AT_FACE + 1, :PAIRS] = pick(face_rank, face_col)
    order[AT_END : AT_END + 1, :] = last_of(face_col)


def kernel(
    pair_count,
    slave_face,
    master_row,
    master_col,
    active,
    coords,
    weights,
    slave_hbm,
    master_hbm,
    out_master,
    out_slave,
    order,
    meta,
    points,
    point_weights,
    window_first,
    window_second,
    slave,
    mortar,
    dual,
    tables,
    first_sq,
    second_sq,
    run,
    mult,
    slave_run,
    send_p,
    recv_p,
    send_o,
    recv_o,
    recv_d,
    send_h,
    recv_h,
    local_sem,
    halo_h_send,
    halo_h_recv,
    halo_p_send,
    halo_p_recv,
    halo_o_send,
    halo_o_recv,
    halo_d_send,
    halo_d_recv,
    halo_f_send,
    halo_f_recv,
    force_l_send,
    force_l_recv,
    force_m_send,
    force_m_recv,
    force_d_send,
    force_d_recv,
    force_h_send,
    force_h_recv,
):
    windows = (window_first, window_second)
    at_len = lax.axis_index("len")
    at_hgt = lax.axis_index("hgt")
    n_len = lax.axis_size("len")
    n_hgt = lax.axis_size("hgt")
    odd = lax.rem(at_len, 2)
    other_len = at_len - 1 + 2 * odd
    partner = (at_len + 1 - 2 * odd, at_hgt)
    other = (lax.rem(other_len + n_len, n_len), at_hgt)
    above = (at_len, lax.rem(at_hgt + 1, n_hgt))
    below = (at_len, lax.rem(at_hgt + n_hgt - 1, n_hgt))
    has_other = (other_len >= 0) & (other_len < n_len)
    has_row = (at_hgt > 0, at_hgt < n_hgt - 1)
    beside = (below, above)
    neighbours = ((partner, None), (other, has_other), (below, has_row[DOWN]), (above, has_row[UP]))

    def when(condition, action):
        if condition is None:
            action()
        else:
            pl.when(condition)(action)

    def remote(src, dst, send_sem, recv_sem, device):
        return pltpu.make_async_remote_copy(
            src_ref=src,
            dst_ref=dst,
            send_sem=send_sem,
            recv_sem=recv_sem,
            device_id=device,
            device_id_type=MESH,
        )

    def faces(g):
        return pl.ds(g * PART, PART)

    def half_of(ref, half, places):
        return ref.at[places, pl.ds(half * ROWS, ROWS)]

    def halo_hgt(half, row, g):
        return remote(
            half_of(master_hbm, half, faces(g)),
            windows[half].at[OWN, 1 - row, faces(g)],
            halo_h_send.at[half, row, g],
            halo_h_recv.at[half, 1 - row, g],
            beside[row],
        )

    def halo_partner(half):
        return remote(
            half_of(master_hbm, half, pl.ds(0, FACES)),
            windows[half].at[PARTNER, MID],
            halo_p_send.at[half],
            halo_p_recv.at[half],
            partner,
        )

    def halo_other(half, g):
        return remote(
            half_of(master_hbm, half, faces(g)),
            windows[half].at[OTHER, MID, faces(g)],
            halo_o_send.at[half, g],
            halo_o_recv.at[half, g],
            other,
        )

    def halo_turn(half, row):
        return remote(
            windows[half].at[OTHER, MID, faces(TURN)],
            windows[half].at[OTHER, 1 - row, faces(TURN)],
            halo_d_send.at[half, row],
            halo_d_recv.at[half, 1 - row],
            beside[row],
        )

    def halo_forward(half, column, row, g):
        return remote(
            windows[half].at[OWN, row, faces(g)],
            windows[half].at[column, row, faces(g)],
            halo_f_send.at[half, column - 1, row, g],
            halo_f_recv.at[half, column - 1, row, g],
            partner if column == PARTNER else other,
        )

    def force_len(half, column, g):
        if column == PARTNER:
            src, dst, device = send_p, recv_p, partner
        else:
            src, dst, device = send_o, recv_o, other
        return remote(
            src.at[half, g, pl.ds(0, 2)],
            dst.at[half, g, pl.ds(0, 2)],
            force_l_send.at[half, column - 1, g],
            force_l_recv.at[half, column - 1, g],
            device,
        )

    def force_mid(half, column, g):
        if column == PARTNER:
            src, dst, device = send_p, recv_p, partner
        else:
            src, dst, device = send_o, recv_o, other
        return remote(
            src.at[half, g, MID],
            dst.at[half, g, MID],
            force_m_send.at[half, column - 1, g],
            force_m_recv.at[half, column - 1, g],
            device,
        )

    def force_turn(half, row):
        return remote(
            send_o.at[half, TURN, row],
            recv_d.at[half, 1 - row],
            force_d_send.at[half, row],
            force_d_recv.at[half, 1 - row],
            beside[row],
        )

    def force_hgt(half, row, g):
        return remote(
            send_h.at[half, row, g],
            recv_h.at[half, 1 - row, g],
            force_h_send.at[half, row, g],
            force_h_recv.at[half, 1 - row, g],
            beside[row],
        )

    def to_other(action):
        pl.when(has_other)(action)

    def to_row(row, action):
        pl.when(has_row[row])(action)

    barrier = pltpu.get_barrier_semaphore()
    for device, there in neighbours:

        def greet(device=device):
            pl.semaphore_signal(barrier, inc=1, device_id=device, device_id_type=MESH)

        when(there, greet)
    loads = [
        pltpu.make_async_copy(coords, points, local_sem.at[0]),
        pltpu.make_async_copy(weights, point_weights, local_sem.at[1]),
        *[
            pltpu.make_async_copy(
                half_of(master_hbm, half, pl.ds(0, FACES)),
                windows[half].at[OWN, MID],
                local_sem.at[2 + half],
            )
            for half in range(HALVES)
        ],
        *[
            pltpu.make_async_copy(
                half_of(slave_hbm, half, pl.ds(0, FACES)), slave.at[half], local_sem.at[4 + half]
            )
            for half in range(HALVES)
        ],
    ]
    for load in loads:
        load.start()
    pl.semaphore_wait(barrier, 1 + sum(there.astype(jnp.int32) for _, there in neighbours[1:]))

    def send_own(half):
        @pl.when(has_other)
        def _():
            for g in (TURN, *range(TURN)):
                halo_other(half, g).start()

        halo_partner(half).start()
        for g in range(CHUNKS):
            for row in (DOWN, UP):
                to_row(row, lambda row=row, g=g: halo_hgt(half, row, g).start())

    send_own(0)
    order_pairs(pair_count, (slave_face, master_row, master_col, active), order)
    publish = pltpu.make_async_copy(order, meta, local_sem.at[6])
    publish.start()
    loads[0].wait()
    loads[1].wait()

    modes = lax.broadcasted_iota(jnp.int32, (ORDER, NODES), 0).astype(F32)
    row_ids = lax.broadcasted_iota(jnp.int32, (NODES, NODES), 0)
    col_ids = lax.broadcasted_iota(jnp.int32, (NODES, NODES), 1)

    def build_tables(first_pair):
        def one(i, _):
            place = points[first_pair + i]
            weight = point_weights[pl.ds(first_pair + i, 1), :]
            sx, sy, mx, my = (cos_pi(modes * place[k : k + 1]) for k in range(4))
            rows = pl.ds(pl.multiple_of((first_pair + i) * ORDER, ORDER), ORDER)
            tables[i, 0] = sx
            tables[i, 1] = sy
            tables[i, 2] = mx * weight
            tables[i, 3] = my
            first_sq[rows, :] = sx * sx * weight
            second_sq[rows, :] = sy * sy
            return 0

        lax.fori_loop(0, GROUP, one, 0)

    def build_dual():
        same_pair = row_ids // ORDER == col_ids // ORDER
        same_node = row_ids % ORDER == col_ids // ORDER
        spread = jnp.where(row_ids % ORDER == col_ids % ORDER, 1.0, 0.0).astype(BF16)
        spread = jnp.concatenate([spread, spread], axis=0)
        for k in range(PAIRS // GROUP):
            rows = pl.ds(k * GROUP * ORDER, GROUP * ORDER)
            high, low = split(first_sq[rows, :])
            left = jnp.concatenate([high, low, high], axis=1)
            high, low = split(second_sq[rows, :])
            right = jnp.concatenate([high, high, low], axis=1)
            sums = lax.dot_general(left, right, NT, preferred_element_type=F32)
            high, low = split(jnp.where(same_pair, sums, 0.0))
            wide = jnp.dot(
                jnp.concatenate([high, low], axis=1), spread, preferred_element_type=F32
            )
            wide = jnp.where(same_node, wide, 0.0)
            dual[k * GROUP : (k + 1) * GROUP, :] = jnp.sum(wide.reshape(GROUP, ORDER, NODES), axis=1)

    def table_of(i, k):
        first, second = tables[i, k], tables[i, k + 1]
        return (first[:, None, :] * second[None, :, :]).reshape(NODES, NODES)

    def build_mortar(first_pair):
        def some(step, _):
            for u in range(LOCK_A):
                i = step * LOCK_A + u
                slave_high, slave_low = split(table_of(i, 0))
                master_high, master_low = split(table_of(i, 2))
                left = jnp.concatenate([slave_high, slave_low, slave_high], axis=1)
                right = jnp.concatenate([master_high, master_high, master_low], axis=1)
                product = lax.dot_general(left, right, NT, preferred_element_type=F32)
                mortar[first_pair + i] = product.astype(BF16)
            return 0

        lax.fori_loop(0, GROUP // LOCK_A, some, 0)

    def relay(half, g):
        @pl.when((g == 0) & has_other)
        def _():
            halo_other(half, TURN).wait_recv()
            for row in (DOWN, UP):
                to_row(row, lambda row=row: halo_turn(half, row).start())

        for row in (DOWN, UP):

            def pass_on(row=row):
                halo_hgt(half, 1 - row, g).wait_recv()
                pl.when(has_other & (g != TURN))(lambda: halo_forward(half, OTHER, row, g).start())
                halo_forward(half, PARTNER, row, g).start()

            to_row(row, pass_on)

    def prepare(g, _):
        build_tables(g * GROUP)
        build_mortar(g * GROUP)
        relay(0, g)
        pl.when(g == CHUNKS - 2)(lambda: send_own(1))
        return 0

    lax.fori_loop(0, CHUNKS, prepare, 0)
    build_dual()

    @pl.when(jnp.logical_not(has_other))
    def _():
        recv_o[...] = jnp.zeros(recv_o.shape, BF16)

    for row in (DOWN, UP):

        @pl.when(jnp.logical_not(has_row[row]))
        def _(row=row):
            for half in range(HALVES):
                recv_h[half, row] = jnp.zeros(recv_h.shape[2:], BF16)
                recv_d[half, row] = jnp.zeros(recv_d.shape[2:], BF16)

    publish.wait()
    for load in loads[2:]:
        load.wait()

    def all_arrived(half):
        halo_partner(half).wait_recv()

        def arrived(g, _):
            pl.when(has_other & (g != TURN))(lambda: halo_other(half, g).wait_recv())
            for row in (DOWN, UP):

                def rest(row=row):
                    halo_forward(half, PARTNER, row, g).wait_recv()
                    pl.when(has_other & (g != TURN))(lambda: halo_forward(half, OTHER, row, g).wait_recv())
                    pl.when(has_other & (g == TURN))(lambda: halo_turn(half, 1 - row).wait_recv())

                to_row(row, rest)
            return 0

        lax.fori_loop(0, CHUNKS, arrived, 0)

    def contact(half, step):
        slots = [step * LOCK_B + u for u in range(LOCK_B)]
        pairs = [meta[AT_PAIR, t] for t in slots]
        keys = [meta[AT_MASTER, t] for t in slots]
        mortars = [mortar[p] for p in pairs]
        projected = []
        for key, matrix in zip(keys, mortars):
            spot = jnp.where(key < SPOTS, key, MID * FACES)
            block = spot // FACES
            master = windows[half][block // 3, block % 3, spot % FACES]
            projected.append(lax.dot_general(master, matrix, NT, preferred_element_type=F32))
        multipliers = []
        for t, p, key, part in zip(slots, pairs, keys, projected):
            diag = dual[pl.ds(p, 1), :]
            gap = slave[half, meta[AT_SLAVE, t]].astype(F32) * diag - part
            multipliers.append(jnp.where(key < SPOTS, gap * (1.0 / diag), 0.0))
        pushes = [
            jnp.dot(m.astype(BF16), matrix, preferred_element_type=F32)
            for m, matrix in zip(multipliers, mortars)
        ]
        for t, m in zip(slots, multipliers):
            mult[half, t] = m
        total = run[half, jnp.maximum(slots[0] - 1, 0)]
        last = meta[AT_MASTER, jnp.maximum(slots[0] - 1, 0)]
        for t, key, push in zip(slots, keys, pushes):
            total = jnp.where(key == last, total, 0.0) + push
            run[half, t] = total
            last = key

    def force(half, column, row, face):
        last = meta[AT_LAST, (column * 3 + row) * FACES + face]
        return jnp.where(last >= 0, run[half, jnp.maximum(last, 0)], 0.0)

    def fill(half, column, g, rows):
        send = send_p if column == PARTNER else send_o
        for row in rows:
            for i in range(PART):
                send[half, g, row, i] = force(half, column, row, g * PART + i).astype(send.dtype)

    def fill_all(half):
        def one(g, _):
            fill(half, OTHER, g, (DOWN, UP))
            fill(half, PARTNER, g, (DOWN, UP, MID))
            pl.when(g != TURN)(lambda: fill(half, OTHER, g, (MID,)))
            return 0

        lax.fori_loop(0, CHUNKS, one, 0)

    def send_all(half):
        for row in (DOWN, UP):
            to_row(row, lambda row=row: force_turn(half, row).start())

        @pl.when(has_other)
        def _():
            for g in range(TURN):
                force_len(half, OTHER, g).start()
            for g in range(TURN):
                force_mid(half, OTHER, g).start()

        for g in (TURN, *range(TURN)):
            force_len(half, PARTNER, g).start()
        for g in range(CHUNKS):
            force_mid(half, PARTNER, g).start()

    def add_slaves(half):
        slave_run[0] = jnp.zeros((ROWS, NODES), F32)

        def some(step, _):
            first = step * LOCK_S
            total = slave_run[jnp.maximum(first - 1, 0)]
            last = meta[AT_FACE, jnp.maximum(first - 1, 0)]
            for u in range(LOCK_S):
                face = meta[AT_FACE, first + u]
                total = jnp.where(face == last, total, 0.0) + mult[half, meta[AT_TURN, first + u]]
                slave_run[first + u] = total
                last = face
            return 0

        lax.fori_loop(0, PAIRS // LOCK_S, some, 0)

        def one(face, _):
            last = meta[AT_END, face]
            total = jnp.where(last >= 0, slave_run[jnp.maximum(last, 0)], 0.0)
            out_slave[face, half * ROWS : (half + 1) * ROWS, :] = total
            return 0

        lax.fori_loop(0, FACES, one, 0)

    def send_heights(half, k):
        g = lax.rem(k + TURN, CHUNKS)
        force_len(half, PARTNER, g).wait_recv()

        def own(row, i):
            return force(half, OWN, row, g * PART + i) + recv_p[half, g, row, i]

        @pl.when(g == TURN)
        def _():
            for row in (DOWN, UP):
                for i in range(PART):
                    send_h[half, row, g, i] = own(row, i).astype(BF16)

        @pl.when(g != TURN)
        def _():
            to_other(lambda: force_len(half, OTHER, g).wait_recv())
            for row in (DOWN, UP):
                for i in range(PART):
                    total = own(row, i) + recv_o[half, g, row, i].astype(F32)
                    send_h[half, row, g, i] = total.astype(BF16)

        for row in (DOWN, UP):
            to_row(row, lambda row=row: force_hgt(half, row, g).start())

        @pl.when(g == TURN)
        def _():
            for row in (DOWN, UP):
                to_row(row, lambda row=row: force_turn(half, 1 - row).wait_recv())
            for i in range(PART):
                total = force(half, OTHER, MID, g * PART + i)
                for row in (DOWN, UP):
                    total = total + recv_d[half, row, i].astype(F32)
                send_o[half, g, MID, i] = total.astype(BF16)
            to_other(lambda: force_mid(half, OTHER, g).start())

    def finish(half, g):
        force_mid(half, PARTNER, g).wait_recv()
        to_other(lambda: force_mid(half, OTHER, g).wait_recv())
        for row in (DOWN, UP):
            to_row(row, lambda row=row: force_hgt(half, 1 - row, g).wait_recv())
        for i in range(PART):
            total = force(half, OWN, MID, g * PART + i)
            total = total + recv_p[half, g, MID, i] + recv_o[half, g, MID, i].astype(F32)
            for row in (DOWN, UP):
                total = total + recv_h[half, row, g, i].astype(F32)
            out_master[g * PART + i, half * ROWS : (half + 1) * ROWS, :] = total

    for half in range(HALVES):
        run[half, 0] = jnp.zeros((ROWS, NODES), F32)

    all_arrived(0)

    def first_half(k, _):
        contact(0, k)
        pl.when(k % 2 == 0)(lambda: relay(1, k // 2))
        return 0

    lax.fori_loop(0, PAIRS // LOCK_B, first_half, 0)
    fill_all(0)
    relay(1, 2)
    send_all(0)
    relay(1, 3)

    all_arrived(1)

    def second_half(k, _):
        contact(1, k)
        send_heights(0, k)
        return 0

    lax.fori_loop(0, PAIRS // LOCK_B, second_half, 0)
    fill_all(1)
    send_all(1)
    for half in range(HALVES):
        add_slaves(half)

    def last_sums(k, _):
        send_heights(1, k)
        finish(0, k)
        return 0

    lax.fori_loop(0, CHUNKS, last_sums, 0)

    def last_faces(g, _):
        finish(1, g)
        return 0

    lax.fori_loop(0, CHUNKS, last_faces, 0)

    for half in range(HALVES):
        halo_partner(half).wait_send()
        for row in (DOWN, UP):
            to_row(row, lambda row=row, half=half: force_turn(half, row).wait_send())
            pl.when(has_row[row] & has_other)(
                lambda row=row, half=half: halo_turn(half, row).wait_send()
            )

        def sent(g, _, half=half):
            to_other(lambda: halo_other(half, g).wait_send())
            force_len(half, PARTNER, g).wait_send()
            force_mid(half, PARTNER, g).wait_send()
            to_other(lambda: force_mid(half, OTHER, g).wait_send())
            pl.when(has_other & (g != TURN))(lambda: force_len(half, OTHER, g).wait_send())
            for row in (DOWN, UP):

                def rest(row=row):
                    halo_hgt(half, row, g).wait_send()
                    force_hgt(half, row, g).wait_send()
                    halo_forward(half, PARTNER, row, g).wait_send()
                    pl.when(has_other & (g != TURN))(lambda: halo_forward(half, OTHER, row, g).wait_send())

                to_row(row, rest)
            return 0

        lax.fori_loop(0, CHUNKS, sent, 0)


def store(master_in, slave_in, master_out, slave_out, sem):
    copies = [
        pltpu.make_async_copy(master_in, master_out, sem.at[0]),
        pltpu.make_async_copy(slave_in, slave_out, sem.at[1]),
    ]
    for copy in copies:
        copy.start()
    for copy in copies:
        copy.wait()


def body(
    slave_disp,
    master_disp,
    quad_coords,
    quad_weights,
    pair_count,
    slave_face,
    master_row,
    master_col,
    active,
):
    face = (CHANNELS, NODES)
    dma = pltpu.SemaphoreType.DMA
    out = jax.ShapeDtypeStruct((FACES, *face), F32)
    held = pltpu.VMEM((FACES, *face), F32)
    vmem = pl.BlockSpec(memory_space=pltpu.VMEM)
    hbm = pl.BlockSpec(memory_space=pl.ANY)
    slots = (1, PAIRS)
    part = (ROWS, NODES)
    results = pl.pallas_call(
        kernel,
        out_shape=(held, held),
        in_specs=[pl.BlockSpec(memory_space=pltpu.SMEM), *[vmem] * 4, *[hbm] * 4],
        out_specs=(vmem, vmem),
        scratch_shapes=[
            pltpu.VMEM(META, jnp.int32),
            pltpu.SMEM(META, jnp.int32),
            pltpu.VMEM((PAIRS, 4, NODES), F32),
            pltpu.VMEM((PAIRS, NODES), F32),
            *[pltpu.VMEM((3, 3, FACES, *part), BF16)] * HALVES,
            pltpu.VMEM((HALVES, FACES, *part), BF16),
            pltpu.VMEM((PAIRS, NODES, NODES), BF16),
            pltpu.VMEM((PAIRS, NODES), F32),
            pltpu.VMEM((GROUP, 4, ORDER, NODES), F32),
            pltpu.VMEM((PAIRS * ORDER, NODES), F32),
            pltpu.VMEM((PAIRS * ORDER, NODES), F32),
            pltpu.VMEM((HALVES, PAIRS, *part), F32),
            pltpu.VMEM((HALVES, PAIRS, *part), F32),
            pltpu.VMEM((PAIRS, *part), F32),
            pltpu.VMEM((HALVES, CHUNKS, 3, PART, *part), F32),
            pltpu.VMEM((HALVES, CHUNKS, 3, PART, *part), F32),
            pltpu.VMEM((HALVES, CHUNKS, 3, PART, *part), BF16),
            pltpu.VMEM((HALVES, CHUNKS, 3, PART, *part), BF16),
            pltpu.VMEM((HALVES, 2, PART, *part), BF16),
            pltpu.VMEM((HALVES, 2, CHUNKS, PART, *part), BF16),
            pltpu.VMEM((HALVES, 2, CHUNKS, PART, *part), BF16),
            dma((7,)),
            *[dma((HALVES, 2, CHUNKS))] * 2,
            *[dma((HALVES,))] * 2,
            *[dma((HALVES, CHUNKS))] * 2,
            *[dma((HALVES, 2))] * 2,
            *[dma((HALVES, 2, 2, CHUNKS))] * 2,
            *[dma((HALVES, 2, CHUNKS))] * 2,
            *[dma((HALVES, 2, CHUNKS))] * 2,
            *[dma((HALVES, 2))] * 2,
            *[dma((HALVES, 2, CHUNKS))] * 2,
        ],
        compiler_params=pltpu.CompilerParams(
            collective_id=0, has_side_effects=True, vmem_limit_bytes=57 * 2**20
        ),
        name="contact",
    )(
        pair_count,
        slave_face.reshape(slots),
        master_row.reshape(slots),
        master_col.reshape(slots),
        active.reshape(slots),
        quad_coords.reshape(PAIRS, 4, NODES),
        quad_weights.reshape(PAIRS, NODES),
        slave_disp.reshape(FACES, *face),
        master_disp.reshape(FACES, *face),
    )
    results = [pltpu.with_memory_space_constraint(r, pltpu.VMEM) for r in results]
    master_force, slave_sum = pl.pallas_call(
        store,
        out_shape=(out, out),
        in_specs=[vmem, vmem],
        out_specs=(hbm, hbm),
        scratch_shapes=[dma((2,))],
        compiler_params=pltpu.CompilerParams(vmem_limit_bytes=2**20),
        name="store",
    )(*results)
    return (
        master_force.reshape(4, 4, *face),
        slave_sum.reshape(4, 4, *face),
    )


def solution(mesh):
    in_specs = (
        P("len", "hgt", None, None),
        P("len", "hgt", None, None),
        P("len", "hgt", None, None, None),
        P("len", "hgt", None, None),
        P("len", "hgt"),
        P("len", "hgt", None),
        P("len", "hgt", None),
        P("len", "hgt", None),
        P("len", "hgt", None),
    )
    out_specs = (P("len", "hgt", None, None), P("len", "hgt", None, None))
    return jax.shard_map(body, mesh=mesh, in_specs=in_specs, out_specs=out_specs, check_vma=False)
```

time: 63.8 us -> 60.3 us (0.945)
  Pallas kernels: 62.4 us -> 58.2 us
    pallas_call x1, Pallas kernels: 60.7 us -> 56.6 us  [body(): pl.pallas_call(kernel, out_shape=(held, held), in_specs=[pl.BlockSpec(mem...]
where the time goes in v3:
time: 60.3 us; the launch traced here: 59.5 us
  Pallas kernels  58.2 us (97%)
  between operations  1.29 us (2%)
    pallas_call x1, Pallas kernels, body(): pl.pallas_call(kernel, out_shape=(held, held), in_specs=[pl.BlockSpec(mem...  56.6 us
    pallas_call x1, Pallas kernels, body(): pl.pallas_call(store, out_shape=(out, out), in_specs=[vmem, vmem], out_sp...  1.68 us

profile of v3, /device:TPU:111, one launch (start us, length us, event | category | flops | bytes accessed | tf_op | source)
XLA Modules:
  0.0 59.5 jit_solution(4764848155220516542)
XLA Ops:
  1.3 56.6 %contact.1 = (f32[16,96,256]{2,1,0:T(8,128)S(1)}, f32[16,96,256]{2,1,0:T(8,128)S(1)}) custom-call(s32[1,1]{1,0:T(1,128)S(6)} %copy.11.pair_count, s32[1,64]{1,0:T(1,128)} %bitcast.14, s32[1,64]{1,0:T(1,128)} %bitcast.15, s32[1,64]{1,0:T(1,128)} %bitcast.16, s32[1,64]{1,0:T(1,128)} %bitcast.17, f32[64,4,256]{2,1,0:T(4,128)} %bitcast.12, f32[64,256]{1,0:T(8,128)} %bitcast.13, ...), custom_call_target="tpu_custom_call" | custom-call | tf_op jit(solution)/shard_map/contact/pallas_call | solution.py:686
  57.8 1.7 %store.1 = (f32[16,96,256]{2,1,0:T(8,128)}, f32[16,96,256]{2,1,0:T(8,128)}) custom-call(f32[16,96,256]{2,1,0:T(8,128)S(1)} %get-tuple-element.6.master_in, f32[16,96,256]{2,1,0:T(8,128)S(1)} %get-tuple-element.7.slave_in), custom_call_target="tpu_custom_call" | custom-call | tf_op jit(solution)/shard_map/store/pallas_call | solution.py:740

commit v4 on v3

--- a/solution.py
+++ b/solution.py
@@ -12,7 +12,8 @@
 CHANNELS = 96
 FACES = 16
 PAIRS = 64
-GROUP = 16
+GROUP = 8
+SQUARES = 16
 LOCK_A = 8
 LOCK_S = 8
 LOCK_B = 16
@@ -357,8 +358,8 @@
         same_node = row_ids % ORDER == col_ids // ORDER
         spread = jnp.where(row_ids % ORDER == col_ids % ORDER, 1.0, 0.0).astype(BF16)
         spread = jnp.concatenate([spread, spread], axis=0)
-        for k in range(PAIRS // GROUP):
-            rows = pl.ds(k * GROUP * ORDER, GROUP * ORDER)
+        for k in range(PAIRS // SQUARES):
+            rows = pl.ds(k * SQUARES * ORDER, SQUARES * ORDER)
             high, low = split(first_sq[rows, :])
             left = jnp.concatenate([high, low, high], axis=1)
             high, low = split(second_sq[rows, :])
@@ -369,7 +370,7 @@
                 jnp.concatenate([high, low], axis=1), spread, preferred_element_type=F32
             )
             wide = jnp.where(same_node, wide, 0.0)
-            dual[k * GROUP : (k + 1) * GROUP, :] = jnp.sum(wide.reshape(GROUP, ORDER, NODES), axis=1)
+            dual[k * SQUARES : (k + 1) * SQUARES, :] = jnp.sum(wide.reshape(SQUARES, ORDER, NODES), axis=1)
 
     def table_of(i, k):
         first, second = tables[i, k], tables[i, k + 1]
@@ -408,11 +409,12 @@
     def prepare(g, _):
         build_tables(g * GROUP)
         build_mortar(g * GROUP)
-        relay(0, g)
-        pl.when(g == CHUNKS - 2)(lambda: send_own(1))
+        for at, chunk in ((1, 0), (4, 2)):
+            pl.when((g == at) | (g == at + 1))(lambda: relay(0, chunk + g - at))
+        pl.when(g == 4)(lambda: send_own(1))
         return 0
 
-    lax.fori_loop(0, CHUNKS, prepare, 0)
+    lax.fori_loop(0, PAIRS // GROUP, prepare, 0)
     build_dual()
 
     @pl.when(jnp.logical_not(has_other))
@@ -487,30 +489,39 @@
             for i in range(PART):
                 send[half, g, row, i] = force(half, column, row, g * PART + i).astype(send.dtype)
 
-    def fill_all(half):
-        def one(g, _):
+    def send_all(half):
+        def side(k, _):
+            g = lax.rem(k + TURN, CHUNKS)
             fill(half, OTHER, g, (DOWN, UP))
-            fill(half, PARTNER, g, (DOWN, UP, MID))
-            pl.when(g != TURN)(lambda: fill(half, OTHER, g, (MID,)))
-            return 0
-
-        lax.fori_loop(0, CHUNKS, one, 0)
-
-    def send_all(half):
-        for row in (DOWN, UP):
-            to_row(row, lambda row=row: force_turn(half, row).start())
-
-        @pl.when(has_other)
-        def _():
-            for g in range(TURN):
-                force_len(half, OTHER, g).start()
-            for g in range(TURN):
-                force_mid(half, OTHER, g).start()
-
-        for g in (TURN, *range(TURN)):
+
+            @pl.when(g == TURN)
+            def _():
+                for row in (DOWN, UP):
+                    to_row(row, lambda row=row: force_turn(half, row).start())
+
+            pl.when(has_other & (g != TURN))(lambda: force_len(half, OTHER, g).start())
+            return 0
+
+        def partner_side(k, _):
+            g = lax.rem(k + TURN, CHUNKS)
+            fill(half, PARTNER, g, (DOWN, UP))
             force_len(half, PARTNER, g).start()
-        for g in range(CHUNKS):
+            return 0
+
+        def middle(g, _):
+            fill(half, OTHER, g, (MID,))
+            to_other(lambda: force_mid(half, OTHER, g).start())
+            return 0
+
+        def partner_middle(g, _):
+            fill(half, PARTNER, g, (MID,))
             force_mid(half, PARTNER, g).start()
+            return 0
+
+        lax.fori_loop(0, CHUNKS, side, 0)
+        lax.fori_loop(0, CHUNKS, partner_side, 0)
+        lax.fori_loop(0, TURN, middle, 0)
+        lax.fori_loop(0, CHUNKS, partner_middle, 0)
 
     def add_slaves(half):
         slave_run[0] = jnp.zeros((ROWS, NODES), F32)
@@ -560,16 +571,15 @@
         for row in (DOWN, UP):
             to_row(row, lambda row=row: force_hgt(half, row, g).start())
 
-        @pl.when(g == TURN)
-        def _():
+    def send_turned(half):
+        for row in (DOWN, UP):
+            to_row(row, lambda row=row: force_turn(half, 1 - row).wait_recv())
+        for i in range(PART):
+            total = force(half, OTHER, MID, TURN * PART + i)
             for row in (DOWN, UP):
-                to_row(row, lambda row=row: force_turn(half, 1 - row).wait_recv())
-            for i in range(PART):
-                total = force(half, OTHER, MID, g * PART + i)
-                for row in (DOWN, UP):
-                    total = total + recv_d[half, row, i].astype(F32)
-                send_o[half, g, MID, i] = total.astype(BF16)
-            to_other(lambda: force_mid(half, OTHER, g).start())
+                total = total + recv_d[half, row, i].astype(F32)
+            send_o[half, TURN, MID, i] = total.astype(BF16)
+        to_other(lambda: force_mid(half, OTHER, TURN).start())
 
     def finish(half, g):
         force_mid(half, PARTNER, g).wait_recv()
@@ -587,15 +597,14 @@
         run[half, 0] = jnp.zeros((ROWS, NODES), F32)
 
     all_arrived(0)
+    relay(1, 0)
 
     def first_half(k, _):
         contact(0, k)
-        pl.when(k % 2 == 0)(lambda: relay(1, k // 2))
+        pl.when(k % 2 == 0)(lambda: relay(1, k // 2 + 1))
         return 0
 
     lax.fori_loop(0, PAIRS // LOCK_B, first_half, 0)
-    fill_all(0)
-    relay(1, 2)
     send_all(0)
     relay(1, 3)
 
@@ -607,13 +616,14 @@
         return 0
 
     lax.fori_loop(0, PAIRS // LOCK_B, second_half, 0)
-    fill_all(1)
+    send_turned(0)
     send_all(1)
     for half in range(HALVES):
         add_slaves(half)
 
     def last_sums(k, _):
         send_heights(1, k)
+        pl.when(k == 2)(lambda: send_turned(1))
         finish(0, k)
         return 0
 

time: 60.3 us -> 58.9 us (0.977)
  Pallas kernels: 58.2 us -> 57.3 us
    pallas_call x1, Pallas kernels: 56.6 us -> 55.7 us  [body(): pl.pallas_call(kernel, out_shape=(held, held), in_specs=[pl.BlockSpec(mem...]
where the time goes in v4:
time: 58.9 us; the launch traced here: 58.6 us
  Pallas kernels  57.3 us (97%)
  between operations  1.29 us (2%)
    pallas_call x1, Pallas kernels, body(): pl.pallas_call(kernel, out_shape=(held, held), in_specs=[pl.BlockSpec(mem...  55.7 us
    pallas_call x1, Pallas kernels, body(): pl.pallas_call(store, out_shape=(out, out), in_specs=[vmem, vmem], out_sp...  1.68 us

profile of v4, /device:TPU:111, one launch (start us, length us, event | category | flops | bytes accessed | tf_op | source)
XLA Modules:
  0.0 58.6 jit_solution(5222130376863381520)
XLA Ops:
  1.3 55.7 %contact.1 = (f32[16,96,256]{2,1,0:T(8,128)S(1)}, f32[16,96,256]{2,1,0:T(8,128)S(1)}) custom-call(s32[1,1]{1,0:T(1,128)S(6)} %copy.11.pair_count, s32[1,64]{1,0:T(1,128)} %bitcast.14, s32[1,64]{1,0:T(1,128)} %bitcast.15, s32[1,64]{1,0:T(1,128)} %bitcast.16, s32[1,64]{1,0:T(1,128)} %bitcast.17, f32[64,4,256]{2,1,0:T(4,128)} %bitcast.12, f32[64,256]{1,0:T(8,128)} %bitcast.13, ...), custom_call_target="tpu_custom_call" | custom-call | tf_op jit(solution)/shard_map/contact/pallas_call | solution.py:696
  56.9 1.7 %store.1 = (f32[16,96,256]{2,1,0:T(8,128)}, f32[16,96,256]{2,1,0:T(8,128)}) custom-call(f32[16,96,256]{2,1,0:T(8,128)S(1)} %get-tuple-element.6.master_in, f32[16,96,256]{2,1,0:T(8,128)S(1)} %get-tuple-element.7.slave_in), custom_call_target="tpu_custom_call" | custom-call | tf_op jit(solution)/shard_map/store/pallas_call | solution.py:750

commit v5 on v4

--- a/solution.py
+++ b/solution.py
@@ -618,22 +618,23 @@
     lax.fori_loop(0, PAIRS // LOCK_B, second_half, 0)
     send_turned(0)
     send_all(1)
-    for half in range(HALVES):
-        add_slaves(half)
 
     def last_sums(k, _):
         send_heights(1, k)
+        for half in range(HALVES):
+            pl.when(k == half)(lambda half=half: add_slaves(half))
         pl.when(k == 2)(lambda: send_turned(1))
-        finish(0, k)
         return 0
 
     lax.fori_loop(0, CHUNKS, last_sums, 0)
 
-    def last_faces(g, _):
-        finish(1, g)
-        return 0
-
-    lax.fori_loop(0, CHUNKS, last_faces, 0)
+    for half in range(HALVES):
+
+        def last_faces(g, _, half=half):
+            finish(half, g)
+            return 0
+
+        lax.fori_loop(0, CHUNKS, last_faces, 0)
 
     for half in range(HALVES):
         halo_partner(half).wait_send()
@@ -664,10 +665,11 @@
 
 
 def store(master_in, slave_in, master_out, slave_out, sem):
-    copies = [
-        pltpu.make_async_copy(master_in, master_out, sem.at[0]),
-        pltpu.make_async_copy(slave_in, slave_out, sem.at[1]),
-    ]
+    copies = []
+    for k in range(CHUNKS):
+        at = pl.ds(k * PART, PART)
+        copies.append(pltpu.make_async_copy(master_in.at[at], master_out.at[at], sem.at[0, k]))
+        copies.append(pltpu.make_async_copy(slave_in.at[at], slave_out.at[at], sem.at[1, k]))
     for copy in copies:
         copy.start()
     for copy in copies:
@@ -752,7 +754,7 @@
         out_shape=(out, out),
         in_specs=[vmem, vmem],
         out_specs=(hbm, hbm),
-        scratch_shapes=[dma((2,))],
+        scratch_shapes=[dma((2, CHUNKS))],
         compiler_params=pltpu.CompilerParams(vmem_limit_bytes=2**20),
         name="store",
     )(*results)

time: 58.9 us -> 58.9 us (level)
  no operation moved by 1% of the time
where the time goes in v5:
time: 58.9 us; the launch traced here: 58.6 us
  Pallas kernels  57.4 us (97%)
  between operations  1.29 us (2%)
    pallas_call x1, Pallas kernels, body(): pl.pallas_call(kernel, out_shape=(held, held), in_specs=[pl.BlockSpec(mem...  55.6 us
    pallas_call x1, Pallas kernels, body(): pl.pallas_call(store, out_shape=(out, out), in_specs=[vmem, vmem], out_sp...  1.72 us

profile of v5, /device:TPU:111, one launch (start us, length us, event | category | flops | bytes accessed | tf_op | source)
XLA Modules:
  0.0 58.6 jit_solution(1506829788233332944)
XLA Ops:
  1.3 55.6 %contact.1 = (f32[16,96,256]{2,1,0:T(8,128)S(1)}, f32[16,96,256]{2,1,0:T(8,128)S(1)}) custom-call(s32[1,1]{1,0:T(1,128)S(6)} %copy.11.pair_count, s32[1,64]{1,0:T(1,128)} %bitcast.14, s32[1,64]{1,0:T(1,128)} %bitcast.15, s32[1,64]{1,0:T(1,128)} %bitcast.16, s32[1,64]{1,0:T(1,128)} %bitcast.17, f32[64,4,256]{2,1,0:T(4,128)} %bitcast.12, f32[64,256]{1,0:T(8,128)} %bitcast.13, ...), custom_call_target="tpu_custom_call" | custom-call | tf_op jit(solution)/shard_map/contact/pallas_call | solution.py:698
  56.9 1.7 %store.1 = (f32[16,96,256]{2,1,0:T(8,128)}, f32[16,96,256]{2,1,0:T(8,128)}) custom-call(f32[16,96,256]{2,1,0:T(8,128)S(1)} %get-tuple-element.6.master_in, f32[16,96,256]{2,1,0:T(8,128)S(1)} %get-tuple-element.7.slave_in), custom_call_target="tpu_custom_call" | custom-call | tf_op jit(solution)/shard_map/store/pallas_call | solution.py:752
